TPU v7x, 32 devices: a whole 2x2x4 slice. The times are simulated.
32 devices in a mesh: rows: 8 (over y, x, core), heads: 4 (over z).
Axes of the slice: x: 2, y: 2, z: 4, core: 2. Of those that a mesh axis runs over, the one named last changes fastest.
Arguments:
- tokens: bfloat16 [8, 2048, 768], P('rows', 'heads'), may hold values from -6 to 6
- segment_ids: int32 [8, 2048], P('rows'), may hold values from 0 to 7, as said below
- w_qkv: bfloat16 [768, 3, 768], P(None, None, 'heads'), may hold values from -0.21875 to 0.21875
- b_qkv: float32 [3, 768], P(None, 'heads'), may hold values from -3 to 3
- w_out: bfloat16 [768, 768], P('heads'), may hold values from -0.75 to 0.75
- b_out: float32 [768], replicated, may hold values from -3 to 3
- gain_one: float32 [768], replicated, may hold values from 0.25 to 1.75
- bias_one: float32 [768], replicated, may hold values from -3 to 3
- w_up: bfloat16 [768, 3072], P(None, 'heads'), may hold values from -0.21875 to 0.21875
- b_up: float32 [3072], P('heads'), may hold values from -3 to 3
- w_down: bfloat16 [3072, 768], P('heads'), may hold values from -0.109375 to 0.109375
- b_down: float32 [768], replicated, may hold values from -3 to 3
- gain_two: float32 [768], replicated, may hold values from 0.25 to 1.75
- bias_two: float32 [768], replicated, may hold values from -3 to 3
- omega: bfloat16 [64, 256], replicated, may hold values from -4 to 4
- cotangent: bfloat16 [8, 2048, 768], P('rows', 'heads'), may hold values from -6 to 6
Outputs:
- layer_output: bfloat16 [8, 2048, 768], P('rows', 'heads')
- grad_tokens: float32 [8, 2048, 768], P('rows', 'heads')
- grad_w_qkv: float32 [768, 3, 768], P(None, None, 'heads')
- grad_b_qkv: float32 [3, 768], P(None, 'heads')
- grad_w_out: float32 [768, 768], P('heads')
- grad_b_out: float32 [768], replicated
- grad_gain_one: float32 [768], replicated
- grad_bias_one: float32 [768], replicated
- grad_w_up: float32 [768, 3072], P(None, 'heads')
- grad_b_up: float32 [3072], P('heads')
- grad_w_down: float32 [3072, 768], P('heads')
- grad_b_down: float32 [768], replicated
- grad_gain_two: float32 [768], replicated
- grad_bias_two: float32 [768], replicated
Inputs may be any that keep to these rules, and one draw needn't show every extreme that they name: `segment_ids`: every row holds all 8 documents, numbered in order of position; each document has at least one position.
All inputs are finite; a program needn't handle non-finite values.
Results may differ from a plain program's by a relative error of at most 0.025.
Values may be sent and summed in bfloat16 or wider, within the bound.
No kernel may reach another device: no remote copies, remote signals or barrier semaphores. Data moves between devices by JAX's collectives and lax.ppermute only.
A program may use at most 192 MiB of HBM per device.

v0:
```python
import jax
import jax.numpy as jnp
from jax import lax
from jax.sharding import PartitionSpec as P

SEGS = 8


EPSILON = 1e-05


def norm_forward(hidden, gain, bias):
    average = jnp.mean(hidden, axis=-1, keepdims=True)
    centred = hidden - average
    inverse = lax.rsqrt(jnp.mean(centred * centred, axis=-1, keepdims=True) + EPSILON)
    normed = centred * inverse
    return (normed * gain + bias, normed, inverse)


def norm_backward(grad_in, normed, inverse, gain):
    scaled = grad_in * gain
    centred = (
        scaled
        - jnp.mean(scaled, axis=-1, keepdims=True)
        - normed * jnp.mean(scaled * normed, axis=-1, keepdims=True)
    )
    return (
        centred * inverse,
        jnp.sum(grad_in * normed, axis=(0, 1)),
        jnp.sum(grad_in, axis=(0, 1)),
    )


def feature_map(vectors, omega, feat_scale, feat_count):
    projected = jnp.einsum("rlhe,em->rlhm", vectors, omega, preferred_element_type=jnp.float32)
    wide_rows = vectors.astype(jnp.float32)
    half_norm = (
        0.5 * feat_scale * feat_scale * jnp.sum(wide_rows * wide_rows, axis=-1, keepdims=True)
    )
    return jnp.exp(feat_scale * projected - half_norm) * feat_count ** (-0.5)


def feature_back(vectors, phi, grad_feat, omega, feat_scale):
    grad_raw = grad_feat * phi
    raw_low = (feat_scale * grad_raw).astype(jnp.bfloat16)
    through = jnp.einsum("rlhm,em->rlhe", raw_low, omega, preferred_element_type=jnp.float32)
    return through - feat_scale * feat_scale * jnp.sum(
        grad_raw, axis=-1, keepdims=True
    ) * vectors.astype(jnp.float32)


def body(
    tokens,
    segment_ids,
    w_qkv,
    b_qkv,
    w_out,
    b_out,
    gain_one,
    bias_one,
    w_up,
    b_up,
    w_down,
    b_down,
    gain_two,
    bias_two,
    omega,
    cotangent,
):
    head_dim, feat_count = omega.shape
    feat_scale = head_dim ** (-0.25)
    full_tokens = lax.all_gather(tokens, "heads", axis=1, tiled=True)
    row_count, length, model_width = full_tokens.shape
    local_cols = w_qkv.shape[2]
    local_heads = local_cols // head_dim
    onehot = (segment_ids[:, :, None] == jnp.arange(SEGS, dtype=jnp.int32)[None, None, :]).astype(
        jnp.float32
    )
    onehot_low = onehot.astype(jnp.bfloat16)
    projected = jnp.einsum("rld,djc->rljc", full_tokens, w_qkv, preferred_element_type=jnp.float32)
    triple = (
        (projected + b_qkv)
        .astype(jnp.bfloat16)
        .reshape(row_count, length, 3, local_heads, head_dim)
    )
    queries = triple[:, :, 0]
    key_rows = triple[:, :, 1]
    values = triple[:, :, 2]
    phi_q = feature_map(queries, omega, feat_scale, feat_count)
    phi_k = feature_map(key_rows, omega, feat_scale, feat_count)
    feat_q = phi_q.astype(jnp.bfloat16)
    feat_k = phi_k.astype(jnp.bfloat16)
    spread = (onehot_low[:, :, None, :, None] * values[:, :, :, None, :]).reshape(
        row_count, length, local_heads, SEGS * head_dim
    )
    state_sums = jnp.einsum(
        "rlhm,rlhc->rhmc", feat_k, spread, preferred_element_type=jnp.float32
    ).astype(jnp.bfloat16)
    state_norms = jnp.einsum(
        "rlhm,rlg->rhmg", feat_k, onehot_low, preferred_element_type=jnp.float32
    ).astype(jnp.bfloat16)
    blocks = jnp.einsum("rlhm,rhmc->rlhc", feat_q, state_sums, preferred_element_type=jnp.float32)
    numerator = jnp.sum(
        blocks.reshape(row_count, length, local_heads, SEGS, head_dim)
        * onehot[:, :, None, :, None],
        axis=3,
    )
    norm_rows = jnp.einsum(
        "rlhm,rhmg->rlhg", feat_q, state_norms, preferred_element_type=jnp.float32
    )
    denominator = jnp.sum(norm_rows * onehot[:, :, None, :], axis=3)
    attended = (
        (numerator / denominator[..., None])
        .astype(jnp.bfloat16)
        .reshape(row_count, length, local_cols)
    )
    attn_terms = jnp.einsum("rlc,cd->rld", attended, w_out, preferred_element_type=jnp.float32)
    mixed = lax.psum_scatter(attn_terms, "heads", scatter_dimension=1, tiled=True) + b_out
    first_out, normed_one, inverse_one = norm_forward(
        tokens.astype(jnp.float32) + mixed, gain_one, bias_one
    )
    full_first = lax.all_gather(first_out.astype(jnp.bfloat16), "heads", axis=1, tiled=True)
    hidden_pre = (
        jnp.einsum("rld,df->rlf", full_first, w_up, preferred_element_type=jnp.float32) + b_up
    )
    activated = jax.nn.gelu(hidden_pre, approximate=False).astype(jnp.bfloat16)
    ffn_terms = jnp.einsum("rlf,fd->rld", activated, w_down, preferred_element_type=jnp.float32)
    ffn_branch = (
        lax.psum_scatter(
            ffn_terms.astype(jnp.bfloat16), "heads", scatter_dimension=1, tiled=True
        ).astype(jnp.float32)
        + b_down
    )
    final_out, normed_two, inverse_two = norm_forward(first_out + ffn_branch, gain_two, bias_two)
    layer_output = final_out.astype(jnp.bfloat16)
    grad_two, grad_gain_two, grad_bias_two = norm_backward(
        cotangent.astype(jnp.float32), normed_two, inverse_two, gain_two
    )
    grad_b_down = jnp.sum(grad_two, axis=(0, 1))
    full_grad_two = lax.all_gather(grad_two.astype(jnp.bfloat16), "heads", axis=1, tiled=True)
    grad_w_down = jnp.einsum(
        "rlf,rld->fd", activated, full_grad_two, preferred_element_type=jnp.float32
    )
    grad_act = jnp.einsum("rld,fd->rlf", full_grad_two, w_down, preferred_element_type=jnp.float32)
    gelu_value, gelu_pull = jax.vjp(lambda v: jax.nn.gelu(v, approximate=False), hidden_pre)
    grad_pre = gelu_pull(grad_act)[0]
    grad_b_up = jnp.sum(grad_pre, axis=(0, 1))
    pre_low = grad_pre.astype(jnp.bfloat16)
    grad_w_up = jnp.einsum("rld,rlf->df", full_first, pre_low, preferred_element_type=jnp.float32)
    first_terms = jnp.einsum("rlf,df->rld", pre_low, w_up, preferred_element_type=jnp.float32)
    grad_first = grad_two + lax.psum_scatter(first_terms, "heads", scatter_dimension=1, tiled=True)
    grad_one, grad_gain_one, grad_bias_one = norm_backward(
        grad_first, normed_one, inverse_one, gain_one
    )
    grad_b_out = jnp.sum(grad_one, axis=(0, 1))
    full_grad_one = lax.all_gather(grad_one.astype(jnp.bfloat16), "heads", axis=1, tiled=True)
    grad_w_out = jnp.einsum(
        "rlc,rld->cd", attended, full_grad_one, preferred_element_type=jnp.float32
    )
    grad_att = jnp.einsum("rld,cd->rlc", full_grad_one, w_out, preferred_element_type=jnp.float32)
    grad_att = grad_att.reshape(row_count, length, local_heads, head_dim)
    grad_num = (grad_att / denominator[..., None]).astype(jnp.bfloat16)
    grad_den = (-jnp.sum(grad_att * numerator, axis=-1) / (denominator * denominator)).astype(
        jnp.bfloat16
    )
    grad_spread = (onehot_low[:, :, None, :, None] * grad_num[:, :, :, None, :]).reshape(
        row_count, length, local_heads, SEGS * head_dim
    )
    grad_norm_rows = onehot_low[:, :, None, :] * grad_den[..., None]
    grad_sums = jnp.einsum(
        "rlhm,rlhc->rhmc", feat_q, grad_spread, preferred_element_type=jnp.float32
    ).astype(jnp.bfloat16)
    grad_norms = jnp.einsum(
        "rlhm,rlhg->rhmg", feat_q, grad_norm_rows, preferred_element_type=jnp.float32
    ).astype(jnp.bfloat16)
    grad_feat_q = jnp.einsum(
        "rlhc,rhmc->rlhm", grad_spread, state_sums, preferred_element_type=jnp.float32
    )
    grad_feat_q = grad_feat_q + jnp.einsum(
        "rlhg,rhmg->rlhm", grad_norm_rows, state_norms, preferred_element_type=jnp.float32
    )
    grad_feat_k = jnp.einsum(
        "rlhc,rhmc->rlhm", spread, grad_sums, preferred_element_type=jnp.float32
    )
    grad_feat_k = grad_feat_k + jnp.einsum(
        "rlg,rhmg->rlhm", onehot_low, grad_norms, preferred_element_type=jnp.float32
    )
    value_blocks = jnp.einsum(
        "rlhm,rhmc->rlhc", feat_k, grad_sums, preferred_element_type=jnp.float32
    )
    grad_values = jnp.sum(
        value_blocks.reshape(row_count, length, local_heads, SEGS, head_dim)
        * onehot[:, :, None, :, None],
        axis=3,
    )
    grad_queries = feature_back(queries, phi_q, grad_feat_q, omega, feat_scale)
    grad_keys = feature_back(key_rows, phi_k, grad_feat_k, omega, feat_scale)
    grad_triple = jnp.stack([grad_queries, grad_keys, grad_values], axis=2).reshape(
        row_count, length, 3, local_cols
    )
    grad_b_qkv = jnp.sum(grad_triple, axis=(0, 1))
    triple_low = grad_triple.astype(jnp.bfloat16)
    grad_w_qkv = jnp.einsum(
        "rld,rljc->djc", full_tokens, triple_low, preferred_element_type=jnp.float32
    )
    input_terms = jnp.einsum("rljc,djc->rld", triple_low, w_qkv, preferred_element_type=jnp.float32)
    grad_tokens = grad_one + lax.psum_scatter(
        input_terms.astype(jnp.bfloat16), "heads", scatter_dimension=1, tiled=True
    ).astype(jnp.float32)
    grad_b_out, grad_gain_one, grad_bias_one, grad_gain_two, grad_bias_two, grad_b_down = lax.psum(
        (grad_b_out, grad_gain_one, grad_bias_one, grad_gain_two, grad_bias_two, grad_b_down),
        "heads",
    )
    (
        grad_w_qkv,
        grad_b_qkv,
        grad_w_out,
        grad_w_up,
        grad_b_up,
        grad_w_down,
        grad_b_out,
        grad_gain_one,
        grad_bias_one,
        grad_gain_two,
        grad_bias_two,
        grad_b_down,
    ) = lax.psum(
        (
            grad_w_qkv,
            grad_b_qkv,
            grad_w_out,
            grad_w_up,
            grad_b_up,
            grad_w_down,
            grad_b_out,
            grad_gain_one,
            grad_bias_one,
            grad_gain_two,
            grad_bias_two,
            grad_b_down,
        ),
        "rows",
    )
    return (
        layer_output,
        grad_tokens,
        grad_w_qkv,
        grad_b_qkv,
        grad_w_out,
        grad_b_out,
        grad_gain_one,
        grad_bias_one,
        grad_w_up,
        grad_b_up,
        grad_w_down,
        grad_b_down,
        grad_gain_two,
        grad_bias_two,
    )


def solution(mesh):
    return jax.shard_map(
        body,
        mesh=mesh,
        in_specs=(
            P("rows", "heads", None),
            P("rows", None),
            P(None, None, "heads"),
            P(None, "heads"),
            P("heads", None),
            P(),
            P(),
            P(),
            P(None, "heads"),
            P("heads"),
            P("heads", None),
            P(),
            P(),
            P(),
            P(),
            P("rows", "heads", None),
        ),
        out_specs=(
            P("rows", "heads", None),
            P("rows", "heads", None),
            P(None, None, "heads"),
            P(None, "heads"),
            P("heads", None),
            P(),
            P(),
            P(),
            P(None, "heads"),
            P("heads"),
            P("heads", None),
            P(),
            P(),
            P(),
        ),
        check_vma=False,
    )
```

profile of v0, /device:TPU:0, one launch (start us, length us, event | category | flops | bytes accessed | tf_op | source)
XLA Modules:
  0.0 879.1 jit_solution(16839042244762672516)
XLA Ops:
  7.2 0.7 all-gather.5.cloned.1.call-update
  8.0 0.7 fusion.68
  8.7 67.1 %all-gather.5.cloned.1.call-done = bf16[1,2048,768]{2,1,0:T(8,128)(2,1)} async-done(((bf16[1,512,768]{2,1,0:T(8,128)(2,1)}), bf16[1,2048,768]{2,1,0:T(8,128)(2,1)}) %all-gather.5.cloned.1.call-update) | async-done | bytes 3145744 | tf_op jit(solution)/shard_map/all_gather | solution.py:72
  75.8 4.2 fusion.29
  81.1 4.3 fusion.8
  85.4 4.2 fusion.7
  89.6 0.9 convolution_convert_fusion.4
  91.3 0.8 copy-done.9
  92.1 1.8 convolution_convert_fusion.2
  94.0 0.8 copy-done.8
  94.8 1.9 fusion.101
  97.2 3.0 multiply_reduce_fusion.1
  100.2 1.5 divide_convert_fusion.1
  101.8 0.9 copy-done.17
  102.7 3.7 convolution_bitcast_fusion
  106.4 109.5 %reduce-scatter.5.cloned.1.call-done = f32[1,512,768]{2,1,0:T(8,128)} async-done(((f32[1,2048,768]{2,1,0:T(8,128)}), f32[1,512,768]{2,1,0:T(8,128)}) %reduce-scatter.5.cloned.1.call-update) | async-done | bytes 1572880 | tf_op jit(solution)/shard_map/reduce_scatter | solution.py:118
  215.9 1.7 fusion.93
  218.0 1.9 fusion.57
  219.9 64.1 %all-gather.7.cloned.1.call-done = bf16[1,2048,768]{2,1,0:T(8,128)(2,1)} async-done(((bf16[1,512,768]{2,1,0:T(8,128)(2,1)}), bf16[1,2048,768]{2,1,0:T(8,128)(2,1)}) %all-gather.7.cloned.1.call-update) | async-done | bytes 3145744 | tf_op jit(solution)/shard_map/all_gather | solution.py:122
  284.1 18.4 %multiply_convert_fusion.2 = (bf16[2048,768]{1,0:T(8,128)(2,1)S(1)}, f32[2048,768]{1,0:T(8,128)}, f32[2048,768]{1,0:T(8,128)}) fusion(f32[768]{0:T(1024)S(1)} %copy-done.60, bf16[768,768]{1,0:T(8,128)(2,1)S(1)} %copy-done, bf16[1,2048,768]{2,1,0:T(8,128)(2,1)} %all-gather.7.cloned.1.call-done), kind=kOutput, calls=%fused_computation.13 | convolution fusion | flops 2519728128 | bytes 20057088 | tf_op jit(solution)/shard_map/rld,df->rlf/dot_general | solution.py:124
  302.5 1.7 copy-done.62
  304.1 4.0 fusion.33
  308.2 59.0 %reduce-scatter.7.cloned.1.call-done = bf16[1,512,768]{2,1,0:T(8,128)(2,1)} async-done(((bf16[1,2048,768]{2,1,0:T(8,128)(2,1)}), bf16[1,512,768]{2,1,0:T(8,128)(2,1)}) %reduce-scatter.7.cloned.1.call-update) | async-done | bytes 786448 | tf_op jit(solution)/shard_map/reduce_scatter | solution.py:129
  367.2 1.7 fusion.91
  369.3 1.3 fusion.50
  370.6 2.3 fusion.88
  372.9 1.1 copy-done.16
  374.0 1.0 convert_element_type.211
  375.5 63.2 %all-gather.9.cloned.1.call-done = bf16[1,2048,768]{2,1,0:T(8,128)(2,1)} async-done(((bf16[1,512,768]{2,1,0:T(8,128)(2,1)}), bf16[1,2048,768]{2,1,0:T(8,128)(2,1)}) %all-gather.9.cloned.1.call-update) | async-done | bytes 3145744 | tf_op jit(solution)/shard_map/all_gather | solution.py:140
  438.7 11.1 %fusion.100 = (f32[768]{0:T(1024)}, bf16[2048,768]{1,0:T(8,128)(2,1)S(1)}) fusion(f32[2048,768]{1,0:T(8,128)} %get-tuple-element.50, bf16[768,768]{1,0:T(8,128)(2,1)} %param.26, bf16[1,2048,768]{2,1,0:T(8,128)(2,1)} %all-gather.9.cloned.1.call-done, f32[2048,768]{1,0:T(8,128)} %get-tuple-element.60, f32[768]{0:T(1024)S(1)} %copy-done.61), kind=kOutput, calls=%fused_computation.151 | convolution fusion | flops 2441084160 | bytes 20060160 | tf_op jit(solution)/shard_map/rld,fd->rlf/dot_general | solution.py:144
  449.8 1.7 copy-done.63
  451.5 4.5 convolution_bitcast_fusion.1
  456.1 109.5 %reduce-scatter.9.cloned.1.call-done = f32[1,512,768]{2,1,0:T(8,128)} async-done(((f32[1,2048,768]{2,1,0:T(8,128)}), f32[1,512,768]{2,1,0:T(8,128)}) %reduce-scatter.9.cloned.1.call-update) | async-done | bytes 1572880 | tf_op jit(solution)/shard_map/reduce_scatter | solution.py:151
  565.6 2.7 multiply_reduce_fusion.2
  568.9 1.1 copy-done.15
  570.0 1.0 convert_element_type.213
  571.2 63.9 %all-gather.11.cloned.1.call-done = bf16[1,2048,768]{2,1,0:T(8,128)(2,1)} async-done(((bf16[1,512,768]{2,1,0:T(8,128)(2,1)}), bf16[1,2048,768]{2,1,0:T(8,128)(2,1)}) %all-gather.11.cloned.1.call-update) | async-done | bytes 3145744 | tf_op jit(solution)/shard_map/all_gather | solution.py:156
  635.2 3.0 fusion.19
  638.3 1.1 copy-done.11
  640.1 1.4 copy-done.3
  641.5 1.8 convolution_convert_fusion.1
  643.3 1.8 fusion.102
  645.2 4.5 fusion.103
  649.6 6.4 fusion.104
  656.8 4.2 fusion.98
  661.0 9.7 %fusion.94 = (f32[2048,3]{0,1:T(4,128)S(1)}, f32[1,2048,3,256]{1,3,2,0:T(8,128)}) fusion(f32[2048,3]{0,1:T(4,128)S(1)} %copy-done.41, f32[2048,3,256]{0,2,1:T(8,128)} %get-tuple-element.57, bf16[2048,3,256]{0,2,1:T(8,128)(2,1)} %copy-done.2, bf16[2048,3]{0,1:T(4,128)(2,1)S(1)} %fusion.81, bf16[2048,8]{0,1:T(8,128)(2,1)S(1)} %copy-done.30, ...), kind=kOutput, calls=%fused_computation.147 | convolution fusion | flops 59817984 | bytes 22114304 | tf_op jit(solution)/shard_map/rlg,rhmg->rlhm/dot_general | solution.py:185
  670.8 6.6 multiply_reduce_fusion
  677.8 1.9 fusion.99
  679.8 0.7 slice-done.6
  681.0 1.9 fusion.97
  683.0 4.0 fusion.34
  687.4 7.1 fusion.21
  694.5 4.2 fusion.25
  698.6 1.7 fusion.17
  700.3 3.2 fusion.54
  704.2 20.2 %all-reduce.2 = (f32[768]{0:T(1024)S(1)}, f32[768]{0:T(1024)S(1)}, f32[768]{0:T(1024)S(1)}, f32[768]{0:T(1024)S(1)}, f32[768]{0:T(1024)S(1)}, /*index=5*/f32[768]{0:T(1024)S(1)}) all-reduce(f32[768]{0:T(1024)S(1)} %get-tuple-element.44, f32[768]{0:T(1024)S(1)} %get-tuple-element.14, ...), channel_id=1, replica_groups=mesh['rows'=8,'heads'=4] {'heads'}, use_global_device_ids=true, to_apply=%region_25.0 | all-reduce | flops 4608 | bytes 36864 | tf_op jit(solution)/shard_map/psum | solution.py:210
  724.4 2.2 maximum_reduce_fusion
  726.6 23.8 %all-reduce = (f32[3,192]{1,0:T(4,128)}, f32[768]{0:T(1024)}, f32[768]{0:T(1024)}, f32[768]{0:T(1024)}, f32[768]{0:T(1024)}, /*index=5*/f32[768]{0:T(1024)}, f32[768]{0:T(1024)}, f32[768]{0:T(1024)}) all-reduce(f32[3,192]{1,0:T(4,128)S(1)} %maximum_reduce_fusion, ...), channel_id=1, replica_groups=mesh['rows'=8,'heads'=4] {'rows'}, use_global_device_ids=true, to_apply=%region_22.0 | all-reduce | flops 5952 | bytes 47616 | tf_op jit(solution)/shard_map/psum | solution.py:227
  750.5 2.9 convert_add_fusion
  753.4 112.1 %all-reduce.5.cloned.1.call-done = (f32[768,3,192]{0,2,1:T(8,128)}, f32[192,768]{1,0:T(8,128)}, f32[768,768]{1,0:T(8,128)}, f32[768,768]{1,0:T(8,128)}) async-done(((f32[768,3,192]{0,2,1:T(8,128)}, f32[192,768]{1,0:T(8,128)}, f32[768,768]{1,0:T(8,128)}, f32[768,768]{1,0:T(8,128)}), (f32[768,3,192]{0,2,1:T(8,128)}, f32[192,768]{1,0:T(8,128)}, f32[768,768]{1,0:T(8,128)}, ...) | async-done | bytes 7077904 | tf_op jit(solution)/shard_map/psum | solution.py:227
  865.5 2.9 copy.69
  868.4 0.8 copy.70
  869.3 1.4 copy.71
  870.7 1.4 copy.72
  (183 shorter events, 8.2 us)
Async XLA Ops:
  7.2 276.9 %copy-start = (bf16[768,768]{1,0:T(8,128)(2,1)S(1)}, bf16[768,768]{1,0:T(8,128)(2,1)}, u32[]{:S(2)}) copy-start(bf16[768,768]{1,0:T(8,128)(2,1)} %param.24) | copy-start | bytes 3538948
  7.2 68.6 %all-gather.5.cloned.1.call-start = ((), (), s32[]{:S(2)}) async-start(), calls=%async_computation.4 | async-start | bytes 3932160 | tf_op jit(solution)/shard_map/all_gather | solution.py:72
  7.9 208.0 %reduce-scatter.5.cloned.1.call-start = ((), (), s32[]{:S(2)}) async-start(), calls=%async_computation.5 | async-start | bytes 7864320 | tf_op jit(solution)/shard_map/reduce_scatter | solution.py:118
  8.7 81.8 %copy-start.29 = (bf16[2048,8]{0,1:T(8,128)(2,1)}, bf16[2048,8]{0,1:T(8,128)(2,1)S(1)}, u32[]{:S(2)}) copy-start(bf16[2048,8]{0,1:T(8,128)(2,1)S(1)} %get-tuple-element.55) | copy-start | bytes 98308
  8.7 88.5 %copy-start.27 = (f32[2048,8]{0,1:T(8,128)}, f32[2048,8]{0,1:T(8,128)S(1)}, u32[]{:S(2)}) copy-start(f32[2048,8]{0,1:T(8,128)S(1)} %get-tuple-element.54) | copy-start | bytes 196612
  75.8 4.2 copy-start.52
  80.3 5.1 copy-start.6
  80.8 4.5 copy-start.42
  80.9 4.5 copy-start.40
  85.4 11.3 %copy-start.2 = (bf16[2048,3,256]{0,2,1:T(8,128)(2,1)}, bf16[2048,3,256]{0,2,1:T(8,128)(2,1)S(1)}, u32[]{:S(2)}) copy-start(bf16[2048,3,256]{0,2,1:T(8,128)(2,1)S(1)} %get-tuple-element.58) | copy-start | bytes 9437188
  85.4 4.2 copy-start.47
  92.1 2.6 copy-start.8
  97.2 3.0 copy-start.38
  97.2 5.4 copy-start.25
  106.3 109.6 %copy-start.21 = (bf16[1,512,768]{2,1,0:T(8,128)(2,1)S(1)}, bf16[1,512,768]{2,1,0:T(8,128)(2,1)}, u32[]{:S(2)}) copy-start(bf16[1,512,768]{2,1,0:T(8,128)(2,1)} %param.16) | copy-start | bytes 2359300
  106.3 109.6 %copy-start.54 = (f32[768]{0:T(1024)S(1)}, f32[768]{0:T(1024)}, u32[]{:S(2)}) copy-start(f32[768]{0:T(1024)} %param.21) | copy-start | bytes 9220
  106.4 177.7 %all-gather.7.cloned.1.call-start = ((), (), s32[]{:S(2)}) async-start(), calls=%async_computation.6 | async-start | bytes 3932160 | tf_op jit(solution)/shard_map/all_gather | solution.py:122
  217.6 66.4 %copy-start.60 = (f32[768]{0:T(1024)S(1)}, f32[768]{0:T(1024)}, u32[]{:S(2)}) copy-start(f32[768]{0:T(1024)} %param.25) | copy-start | bytes 9220
  217.9 84.5 %copy-start.45 = (f32[512]{0:T(512)}, f32[512]{0:T(512)S(1)}, u32[]{:S(2)}) copy-start(f32[512]{0:T(512)S(1)} %add_rsqrt_fusion.1) | copy-start | bytes 6148
  219.9 147.3 %reduce-scatter.7.cloned.1.call-start = ((), (), s32[]{:S(2)}) async-start(), calls=%async_computation.7 | async-start | bytes 3932160 | tf_op jit(solution)/shard_map/reduce_scatter | solution.py:129
  284.1 20.1 %copy-start.58 = (bf16[768,768]{1,0:T(8,128)(2,1)S(1)}, bf16[768,768]{1,0:T(8,128)(2,1)}, u32[]{:S(2)}) copy-start(bf16[768,768]{1,0:T(8,128)(2,1)} %param.26) | copy-start | bytes 3538948
  308.1 61.1 %copy-start.22 = (bf16[1,512,768]{2,1,0:T(8,128)(2,1)S(1)}, bf16[1,512,768]{2,1,0:T(8,128)(2,1)}, u32[]{:S(2)}) copy-start(bf16[1,512,768]{2,1,0:T(8,128)(2,1)} %param.31) | copy-start | bytes 2359300
  308.2 130.6 %all-gather.9.cloned.1.call-start = ((), (), s32[]{:S(2)}) async-start(), calls=%async_computation.8 | async-start | bytes 3932160 | tf_op jit(solution)/shard_map/all_gather | solution.py:140
  367.2 2.1 copy-start.50
  367.2 3.4 copy-start.55
  372.9 65.8 %copy-start.61 = (f32[768]{0:T(1024)S(1)}, f32[768]{0:T(1024)}, u32[]{:S(2)}) copy-start(f32[768]{0:T(1024)} %param.25) | copy-start | bytes 9220
  375.1 190.5 %reduce-scatter.9.cloned.1.call-start = ((), (), s32[]{:S(2)}) async-start(), calls=%async_computation.9 | async-start | bytes 7864320 | tf_op jit(solution)/shard_map/reduce_scatter | solution.py:151
  456.0 109.6 %copy-start.44 = (f32[768]{0:T(1024)S(1)}, f32[768]{0:T(1024)}, u32[]{:S(2)}) copy-start(f32[768]{0:T(1024)} %param.22) | copy-start | bytes 9220
  456.0 109.6 %copy-start.46 = (f32[512]{0:T(512)S(1)}, f32[512]{0:T(512)}, u32[]{:S(2)}) copy-start(f32[512]{0:T(512)} %copy-done.45) | copy-start | bytes 6148
  456.0 179.2 %all-gather.11.cloned.1.call-start = ((), (), s32[]{:S(2)}) async-start(), calls=%async_computation.10 | async-start | bytes 3932160 | tf_op jit(solution)/shard_map/all_gather | solution.py:156
  568.3 66.8 %copy-start.26 = (bf16[192,768]{1,0:T(8,128)(2,1)S(1)}, bf16[192,768]{1,0:T(8,128)(2,1)}, u32[]{:S(2)}) copy-start(bf16[192,768]{1,0:T(8,128)(2,1)} %param.20) | copy-start | bytes 884740
  571.0 68.4 %copy-start.39 = (f32[2048,3]{0,1:T(4,128)S(1)}, f32[2048,3]{0,1:T(4,128)}, u32[]{:S(2)}) copy-start(f32[2048,3]{0,1:T(4,128)} %copy-done.38) | copy-start | bytes 73732
  571.0 68.5 %copy-start.10 = (bf16[2048,8,64]{0,2,1:T(8,128)(2,1)S(1)}, bf16[2048,8,64]{0,2,1:T(8,128)(2,1)}, u32[]{:S(2)}) copy-start(bf16[2048,8,64]{0,2,1:T(8,128)(2,1)} %copy-done.9) | copy-start | bytes 6291460
  571.0 179.4 %reduce-scatter.11.cloned.1.call-start = ((), (), s32[]{:S(2)}) async-start(), calls=%async_computation.11 | async-start | bytes 3932160 | tf_op jit(solution)/shard_map/reduce_scatter | solution.py:207
  639.6 1.9 copy-start.3
  639.6 5.5 slice-start
  641.4 3.7 slice-start.1
  645.1 4.5 copy-start.5
  645.1 11.2 %slice-start.2 = ((s8[6291456]{0:T(1024)(128)(4,1)}), s8[4194304]{0:T(1024)(128)(4,1)S(1)}, s32[]{:S(2)}) async-start(s8[6291456]{0:T(1024)(128)(4,1)} %bitcast.192), calls=%async_computation.15 | async-start | bytes 8388608
  649.6 6.4 copy-start.12
  649.6 6.4 copy-start.14
  649.6 6.7 slice-start.3
  656.8 4.2 copy-start.41
  661.0 9.7 %copy-start.28 = (f32[2048,8]{0,1:T(8,128)S(1)}, f32[2048,8]{0,1:T(8,128)}, u32[]{:S(2)}) copy-start(f32[2048,8]{0,1:T(8,128)} %copy-done.27) | copy-start | bytes 196612
  670.7 6.8 slice-start.4
  670.7 6.8 copy-start.7
  670.7 7.1 slice-start.5
  670.8 7.1 copy-start.37
  677.3 3.1 slice-start.6
  677.5 5.5 copy-start.33
  677.8 3.2 slice-start.7
  681.0 2.0 copy-start.59
  683.0 4.1 copy-start.31
  687.0 178.4 %all-reduce.5.cloned.1.call-start = ((), (), s32[]{:S(2)}) async-start(), calls=%async_computation.12 | async-start | bytes 14155776 | tf_op jit(solution)/shard_map/psum | solution.py:227
  687.3 7.1 copy-start.57
  687.4 7.1 copy-start.64
  694.4 4.2 copy-start.13
  694.4 4.2 copy-start.18
  694.4 5.9 copy-start.56
  703.6 23.1 %copy-start.53 = (f32[768]{0:T(1024)S(1)}, f32[768]{0:T(1024)}, u32[]{:S(2)}) copy-start(f32[768]{0:T(1024)} %get-tuple-element.69) | copy-start | bytes 9220
  865.5 3.0 copy-start.35
  865.5 3.8 copy-start.24
  868.4 2.2 copy-start.23
  869.3 2.8 copy-start.1
  (18 other events, 22.2 us)
Sparse Core Ops, SparseCore 0:
  9.6 66.1 all-gather.4
  106.5 109.3 reduce-scatter.4
  220.0 64.0 all-gather.6
  308.3 58.8 reduce-scatter.6
  375.2 63.5 all-gather.8
  456.2 109.3 reduce-scatter.8
  571.1 64.0 all-gather.10
  687.2 59.9 reduce-scatter.10
  752.0 113.4 all-reduce.4
where the time goes:
time: 888 us; the launch traced here: 879 us
  waiting for transfers between devices  649 us (73%)
  matrix products  115 us (13%)
  blocking collectives  44 us (5%)
  other arithmetic  34 us (4%)
  local copies, waits for them, and re-layouts  20.7 us (2%)
  between operations  15 us (2%)
    psum x1, waiting for transfers between devices, body(): lax.psum((grad_w_qkv, grad_b_qkv, grad_w_out, grad_w_up, grad_b_up, grad_...  112 us
    reduce_scatter x1, waiting for transfers between devices, body(): lax.psum_scatter(first_terms, 'heads', scatter_dimension=1, tiled=True)  110 us
    reduce_scatter x1, waiting for transfers between devices, body(): lax.psum_scatter(attn_terms, 'heads', scatter_dimension=1, tiled=True)  110 us
    all_gather x1, waiting for transfers between devices, body(): full_tokens = lax.all_gather(tokens, 'heads', axis=1, tiled=True)  67.1 us
    all_gather x1, waiting for transfers between devices, body(): lax.all_gather(first_out.astype(jnp.bfloat16), 'heads', axis=1, tiled=True)  64.1 us
    all_gather x1, waiting for transfers between devices, body(): lax.all_gather(grad_one.astype(jnp.bfloat16), 'heads', axis=1, tiled=True)  63.9 us
    all_gather x1, waiting for transfers between devices, body(): lax.all_gather(grad_two.astype(jnp.bfloat16), 'heads', axis=1, tiled=True)  63.2 us
    reduce_scatter x1, waiting for transfers between devices, body(): lax.psum_scatter(ffn_terms.astype(jnp.bfloat16), 'heads', scatter_dimensi...  59 us
  transfers between devices with their start and end apart: 9, of which 8 were waited for; matrix products, arithmetic and copies ran while one was open for 2% of the time, Pallas kernels for 0%

commit v1 on v0

v1 whole, which is shorter than its diff:
```python
import functools

import jax
import jax.numpy as jnp
from jax import lax
from jax.experimental import pallas as pl
from jax.experimental.pallas import tpu as pltpu
from jax.sharding import PartitionSpec as P

EPSILON = 1e-05
PLANE = 8
VMEM_LIMIT = 48 * 1024 * 1024
BF = jnp.bfloat16
F32 = jnp.float32


def dot(a, b, dims=((1,), (0,))):
    return lax.dot_general(a, b, (dims, ((), ())), preferred_element_type=F32)


def dot_nt(a, b):
    return dot(a, b, ((1,), (1,)))


def dot_tn(a, b):
    return dot(a, b, ((0,), (0,)))


def estimate(us):
    return pl.CostEstimate(flops=int(us * 1.1e9), bytes_accessed=0, transcendentals=0)


def call(kernel, grid, in_specs, out_specs, out_shape, args, us, scratch=()):
    return pl.pallas_call(
        kernel,
        grid=grid,
        in_specs=in_specs,
        out_specs=out_specs,
        out_shape=out_shape,
        scratch_shapes=list(scratch),
        compiler_params=pltpu.CompilerParams(vmem_limit_bytes=VMEM_LIMIT),
        cost_estimate=estimate(us),
    )(*args)


def whole(*shape):
    return pl.BlockSpec(shape, lambda g: (0,) * len(shape))


def part(*shape):
    return pl.BlockSpec((None, *shape), lambda g: (g,) + (0,) * len(shape))


def struct(shape, dtype):
    return jax.ShapeDtypeStruct(shape, dtype)


def permute(array, axis, size, partner):
    return lax.ppermute(array, axis, [(i, partner(i)) for i in range(size)])


def first_partner(i):
    return i ^ (4 if i & 1 else 2)


def second_partner(i):
    return i ^ (2 if i & 1 else 4)


def core_partner(i):
    return i ^ 1


def plane_gather(piece, rows):
    p0 = piece
    p1 = permute(p0, "rows", rows, first_partner)
    p2 = permute(p0, "rows", rows, second_partner)
    p3 = permute(p1, "rows", rows, second_partner)
    own = [p0, p1, p2, p3]
    return own + [permute(p, "rows", rows, core_partner) for p in own]


def plane_slots(rank):
    me = rank & (PLANE - 1)
    core = rank & 1
    first = jnp.where(core == 1, 4, 2)
    second = jnp.where(core == 1, 2, 4)
    return [
        me,
        me ^ first,
        me ^ second,
        me ^ 6,
        me ^ 1,
        me ^ 1 ^ second,
        me ^ 1 ^ first,
        me ^ 7,
    ]


def to_heads(array):
    return lax.all_to_all(array, "heads", 0, 0, tiled=True)


def reduce_grads(sent, kept, rank, rows):
    came = permute(sent, "rows", rows, core_partner)
    core = rank & 1
    mine = (rank & (PLANE - 1)) >> 1
    first = jnp.where(core == 1, 2, 1)
    second = jnp.where(core == 1, 1, 2)

    def pick(slot):
        a = lax.dynamic_index_in_dim(kept, slot, 1, keepdims=False)
        b = lax.dynamic_index_in_dim(came, slot, 1, keepdims=False)
        return a.astype(F32) + b.astype(F32)

    sent = jnp.stack([pick(mine ^ second), pick(mine ^ 3)]).astype(BF)
    came2 = permute(sent, "rows", rows, second_partner)
    sent = (pick(mine ^ first) + came2[1].astype(F32)).astype(BF)
    came3 = permute(sent, "rows", rows, first_partner)
    total = pick(mine) + came2[0].astype(F32) + came3.astype(F32)
    mask = PLANE
    while mask < rows:
        total = total + permute(
            total.astype(BF), "rows", rows, lambda i, m=mask: i ^ m
        ).astype(F32)
        mask *= 2
    total = to_heads(total.astype(BF)).astype(F32)
    return plane_gather(jnp.sum(total, axis=0).astype(BF), rows)


SMEM_SPEC = pl.BlockSpec(memory_space=pltpu.SMEM)
VMEM_SPEC = pl.BlockSpec(memory_space=pltpu.VMEM)


def place_weights_kernel(count, parts, info_ref, *refs):
    owns = refs[:parts]
    pieces = refs[parts : parts + count]
    outs = refs[parts + count :]
    step = pieces[0].shape[0] // parts
    mine = pl.program_id(0) == info_ref[count]

    @pl.when(mine)
    def _():
        for own, out in zip(owns, outs):
            out[...] = own[...]

    @pl.when(jnp.logical_not(mine))
    def _():
        for n in range(count):
            start = pl.multiple_of(info_ref[n] * step, 16)
            for p, out in enumerate(outs):
                out[pl.ds(start, step), :] = pieces[n][p * step : (p + 1) * step, :]


def place_weights(owns, pieces, info):
    count, parts = len(pieces), len(owns)
    others, rows, cols = pieces[0].shape
    height = owns[0].shape[0]

    def piece_index(g, info_ref):
        return (jnp.maximum((g ^ info_ref[count]) - 1, 0), 0, 0)

    return pl.pallas_call(
        functools.partial(place_weights_kernel, count, parts),
        grid_spec=pltpu.PrefetchScalarGridSpec(
            num_scalar_prefetch=1,
            grid=(others + 1,),
            in_specs=[pl.BlockSpec((height, cols), lambda g, s: (0, 0))] * parts
            + [pl.BlockSpec((None, rows, cols), piece_index)] * count,
            out_specs=[pl.BlockSpec((None, height, cols), lambda g, s: (g, 0, 0))] * parts,
        ),
        out_shape=[struct((others + 1, height, cols), BF)] * parts,
        compiler_params=pltpu.CompilerParams(vmem_limit_bytes=VMEM_LIMIT),
        cost_estimate=estimate(3 * parts),
    )(info, *owns, *pieces)


def place_ffn_kernel(count, info_ref, *refs):
    up, down = refs[count], refs[count + 1]
    step = refs[0].shape[0] // 2
    for n in range(count):
        start = pl.multiple_of(info_ref[n] * step, 16)
        up[pl.ds(start, step), :] = refs[n][:step, :].astype(F32)
        down[pl.ds(start, step), :] = refs[n][step:, :].astype(F32)


def place_ffn(pieces, info):
    rows, cols = pieces[0].shape
    count = len(pieces)
    return pl.pallas_call(
        functools.partial(place_ffn_kernel, count),
        in_specs=[SMEM_SPEC] + [VMEM_SPEC] * count,
        out_specs=[VMEM_SPEC] * 2,
        out_shape=[struct((count * rows // 2, cols), F32)] * 2,
        compiler_params=pltpu.CompilerParams(vmem_limit_bytes=VMEM_LIMIT),
        cost_estimate=estimate(4),
    )(info, *pieces)


def place_attention_kernel(count, cols, width, info_ref, *refs):
    qo, kv = refs[:count], refs[count : 2 * count]
    out_qkv, out_o, bias = refs[2 * count :]
    step = qo[0].shape[0]
    for n in range(count):
        start = pl.multiple_of(info_ref[n] * step, 16)
        wide = qo[n][...].astype(F32)

        @pl.when(start < cols)
        def _():
            out_qkv[pl.ds(start, step), :] = wide[:, :width]
            bias[pl.ds(start, step), :] = wide[:, width:]

        @pl.when(start >= cols)
        def _():
            out_o[pl.ds(pl.multiple_of(start - cols, 16), step), :] = wide[:, :width]

        wide = kv[n][...].astype(F32)
        out_qkv[pl.ds(cols + start, step), :] = wide[:, :width]
        bias[pl.ds(cols + start, step), :] = wide[:, width:]


def place_attention(qo, kv, info, cols, width):
    count = len(qo)
    return pl.pallas_call(
        functools.partial(place_attention_kernel, count, cols, width),
        in_specs=[SMEM_SPEC] + [VMEM_SPEC] * (2 * count),
        out_specs=[VMEM_SPEC] * 3,
        out_shape=[struct((3 * cols, width), F32), struct((cols, width), F32), struct((3 * cols, 128), F32)],
        compiler_params=pltpu.CompilerParams(vmem_limit_bytes=VMEM_LIMIT),
        cost_estimate=estimate(3),
    )(info, *qo, *kv)


def phi_of(raw, vectors, head, hd, feats, scale):
    wide = vectors[:, head * hd : (head + 1) * hd].astype(F32)
    half = 0.5 * scale * scale * jnp.sum(wide * wide, axis=-1, keepdims=True)
    part_raw = raw[:, head * feats : (head + 1) * feats]
    return jnp.exp(scale * part_raw - half) * feats ** (-0.5)


def edge_rows(first, last, head):
    lane = lax.broadcasted_iota(jnp.int32, (first.shape[0], 32), 1)
    return jnp.where(lane == head, first, 0.0) + jnp.where(lane == 16 + head, last, 0.0)


def edge_left(value, norm, first, last, head):
    return jnp.concatenate(
        [value * first, value * last, edge_rows(norm * first, norm * last, head)], axis=1
    ).astype(BF)


def put_edges(edge_ref, states, heads, hd, level):
    cols = heads * hd
    norms = states[0][2 * hd :]
    for state in states[1:]:
        norms = norms + state[2 * hd :]
    firsts = jnp.concatenate([s[:hd] for s in states] + [norms[:16]], axis=0).astype(BF)
    lasts = jnp.concatenate([s[hd : 2 * hd] for s in states] + [norms[16:]], axis=0).astype(BF)
    for m in range(edge_ref.shape[0]):

        @pl.when(m > level)
        def _():
            edge_ref[m] = lasts

        @pl.when(m <= level)
        def _():
            edge_ref[m] = firsts


def take_edges(came_ref, match_ref):
    left = right = None
    count = came_ref.shape[0]
    for m in range(count):
        wide = came_ref[m].astype(F32)
        a, b = wide * match_ref[m], wide * match_ref[count + m]
        left = a if left is None else left + a
        right = b if right is None else right + b
    return left.astype(BF), right.astype(BF)


def stack_edges(f, l, h, hd, cols):
    return jnp.concatenate(
        [f[h * hd : (h + 1) * hd], l[h * hd : (h + 1) * hd], f[cols:], l[cols:]], axis=0
    )


def with_one(value):
    lane = lax.broadcasted_iota(jnp.int32, value.shape, 1)
    return jnp.concatenate([value, jnp.where(lane == 0, 1.0, 0.0).astype(value.dtype)], axis=1)


def keys_kernel(heads, hd, feats, info_ref, x_ref, w_ref, b_ref, om_ref, ends_ref, kv_ref, phi_ref, edge_ref):
    cols = heads * hd
    scale = hd ** (-0.25)
    kv = (dot_nt(x_ref[...], w_ref[...]) + b_ref[...]).astype(BF)
    kv_ref[...] = kv
    raw = dot(kv[:, :cols], om_ref[...])
    first, last = ends_ref[:, 0:1], ends_ref[:, 1:2]
    states = []
    for h in range(heads):
        phi = phi_of(raw, kv, h, hd, feats, scale).astype(BF)
        phi_ref[:, h * feats : (h + 1) * feats] = phi
        value = kv[:, cols + h * hd : cols + (h + 1) * hd].astype(F32)
        states.append(dot_tn(edge_left(value, 1.0, first, last, h), phi))
    put_edges(edge_ref, states, heads, hd, info_ref[PLANE])


def queries_kernel(
    heads, hd, feats, x_ref, w_ref, b_ref, om_ref, same_ref, kv_ref, phik_ref, q_ref, phi_ref, nd_ref
):
    cols = heads * hd
    scale = hd ** (-0.25)
    q = (dot_nt(x_ref[...], w_ref[:cols, :]) + b_ref[...]).astype(BF)
    q_ref[...] = q
    raw = dot(q, om_ref[...])
    same = same_ref[...]
    for h in range(heads):
        phi = phi_of(raw, q, h, hd, feats, scale).astype(BF)
        phi_ref[:, h * feats : (h + 1) * feats] = phi
        scores = dot_nt(phi, phik_ref[:, h * feats : (h + 1) * feats]).astype(BF) * same
        value = kv_ref[:, cols + h * hd : cols + (h + 1) * hd]
        nd_ref[:, 2 * h * hd : 2 * (h + 1) * hd] = dot(scores, with_one(value))


def attend_kernel(
    heads, hd, feats, match_ref, phi_ref, nd_ref, came_ref, ends_ref, w_ref, x_ref, bias_ref, vec_ref,
    att_ref, den_ref, cf_ref, cl_ref, normed_ref, inverse_ref, low_ref, acc_ref,
):
    g = pl.program_id(0)
    cols = heads * hd
    first, last = ends_ref[:, 0:1], ends_ref[:, 1:2]
    lane = lax.broadcasted_iota(jnp.int32, den_ref.shape, 1)
    dens = jnp.zeros(den_ref.shape, F32)
    outs = []
    cf, cl = take_edges(came_ref, match_ref)
    cf_ref[...] = cf
    cl_ref[...] = cl
    for h in range(heads):
        far = dot_nt(phi_ref[:, h * feats : (h + 1) * feats], stack_edges(cf, cl, h, hd, cols))
        nd = nd_ref[:, 2 * h * hd : 2 * (h + 1) * hd]
        num = nd[:, :hd] + first * far[:, :hd] + last * far[:, hd : 2 * hd]
        den = (
            nd[:, hd : hd + 1]
            + first * far[:, 2 * hd + h : 2 * hd + h + 1]
            + last * far[:, 2 * hd + 16 + h : 2 * hd + 17 + h]
        )
        outs.append(num / den)
        dens = dens + jnp.where(lane == h, den, 0.0)
    att = jnp.concatenate(outs, axis=1).astype(BF)
    att_ref[...] = att
    den_ref[...] = dens
    mixed = dot(att, w_ref[cols:, :])

    @pl.when(g == 0)
    def _():
        acc_ref[...] = x_ref[...].astype(F32) + bias_ref[...] + mixed

    @pl.when(g > 0)
    def _():
        acc_ref[...] += mixed

    @pl.when(g == pl.num_programs(0) - 1)
    def _():
        normed, inverse = norm_of(acc_ref[...])
        normed_ref[...] = normed
        inverse_ref[...] = jnp.broadcast_to(inverse, inverse_ref.shape)
        low_ref[...] = (normed * vec_ref[0:1, :] + vec_ref[1:2, :]).astype(BF)


def attend_back_kernel(
    heads, hd, feats, info_ref, dh_ref, w_ref, att_ref, den_ref, phi_ref, ends_ref, dnd_ref, edge_ref
):
    cols = heads * hd
    first, last = ends_ref[:, 0:1], ends_ref[:, 1:2]
    datt = dot_nt(dh_ref[...], w_ref[cols:, :])
    lane = lax.broadcasted_iota(jnp.int32, (datt.shape[0], hd), 1)
    states = []
    for h in range(heads):
        inverse = 1.0 / den_ref[:, h : h + 1]
        part_datt = datt[:, h * hd : (h + 1) * hd]
        att = att_ref[:, h * hd : (h + 1) * hd].astype(F32)
        dnum = part_datt * inverse
        dden = -jnp.sum(part_datt * att, axis=-1, keepdims=True) * inverse
        dnd_ref[:, 2 * h * hd : 2 * (h + 1) * hd] = jnp.concatenate(
            [dnum, jnp.where(lane == 0, dden, 0.0)], axis=1
        ).astype(BF)
        states.append(
            dot_tn(edge_left(dnum, dden, first, last, h), phi_ref[:, h * feats : (h + 1) * feats])
        )
    put_edges(edge_ref, states, heads, hd, info_ref[PLANE])


def feature_back(dphi, phi, vectors, om, heads, hd, feats, scale):
    lows, sums = [], []
    for h in range(heads):
        grad_raw = dphi[h] * phi[:, h * feats : (h + 1) * feats].astype(F32)
        lows.append((scale * grad_raw).astype(BF))
        total = jnp.sum(grad_raw, axis=-1, keepdims=True)
        sums.append(total * vectors[:, h * hd : (h + 1) * hd].astype(F32))
    through = dot_nt(jnp.concatenate(lows, axis=1), om)
    return through - scale * scale * jnp.concatenate(sums, axis=1)


def put_slices(source_ref, base, sent_ref, kept_ref, core):
    step = source_ref.shape[0] // PLANE
    for i in range(PLANE // 2):
        other = pl.multiple_of((2 * i + 1 - core) * step, 16)
        own = pl.multiple_of((2 * i + core) * step, 16)
        sent_ref[i, base : base + step, :] = source_ref[pl.ds(other, step), :]
        kept_ref[i, base : base + step, :] = source_ref[pl.ds(own, step), :]


def queries_back_kernel(
    heads, hd, feats, info_ref, dnd_ref, q_ref, phiq_ref, kv_ref, phik_ref, cf_ref, cl_ref, om_ref, same_ref,
    ends_ref, att_ref, x_ref, one_ref, dq_ref, dphik_ref, dv_ref, sent_ref, kept_ref, grad_ref,
):
    cols = heads * hd
    scale = hd ** (-0.25)
    first, last = ends_ref[:, 0:1], ends_ref[:, 1:2]
    same = same_ref[...]
    dphis, dvs = [], []
    for h in range(heads):
        phiq = phiq_ref[:, h * feats : (h + 1) * feats]
        phik = phik_ref[:, h * feats : (h + 1) * feats]
        value = with_one(kv_ref[:, cols + h * hd : cols + (h + 1) * hd])
        dnd = dnd_ref[:, 2 * h * hd : 2 * (h + 1) * hd]
        dscore = dot_nt(dnd, value).astype(BF) * same
        dscore_t = dot_nt(value, dnd).astype(BF) * same
        score_t = dot_nt(phik, phiq).astype(BF) * same
        wide = dnd.astype(F32)
        left = edge_left(wide[:, :hd], wide[:, hd : hd + 1], first, last, h)
        stack = stack_edges(cf_ref[...], cl_ref[...], h, hd, cols)
        dphis.append(dot(dscore, phik) + dot(left, stack))
        dphik_ref[:, h * feats : (h + 1) * feats] = dot(dscore_t, phiq)
        dvs.append(dot(score_t, dnd)[:, :hd])
    dv_ref[...] = jnp.concatenate(dvs, axis=1)
    dq = feature_back(dphis, phiq_ref[...], q_ref[...], om_ref[...], heads, hd, feats, scale)
    dq = dq.astype(BF)
    dq_ref[...] = dq
    grad_ref[:cols, :] = dot_tn(dq, x_ref[...]).astype(BF)
    grad_ref[cols:, :] = dot_tn(att_ref[...], one_ref[...]).astype(BF)
    put_slices(grad_ref, 0, sent_ref, kept_ref, info_ref[0] & 1)


def keys_back_kernel(
    heads, hd, feats, info_ref, match_ref, kv_ref, phik_ref, dphik_ref, dv_ref, came_ref, om_ref, ends_ref, x_ref,
    dkv_ref, sent_ref, kept_ref, grad_ref,
):
    cols = heads * hd
    scale = hd ** (-0.25)
    first, last = ends_ref[:, 0:1], ends_ref[:, 1:2]
    rf, rl = take_edges(came_ref, match_ref)
    dphis, dvs = [], []
    for h in range(heads):
        phik = phik_ref[:, h * feats : (h + 1) * feats]
        value = kv_ref[:, cols + h * hd : cols + (h + 1) * hd].astype(F32)
        stack = stack_edges(rf, rl, h, hd, cols)
        dphis.append(
            dphik_ref[:, h * feats : (h + 1) * feats] + dot(edge_left(value, 1.0, first, last, h), stack)
        )
        far = dot_nt(phik, stack[: 2 * hd])
        dvs.append(dv_ref[:, h * hd : (h + 1) * hd] + first * far[:, :hd] + last * far[:, hd:])
    dk = feature_back(dphis, phik_ref[...], kv_ref[:, :cols], om_ref[...], heads, hd, feats, scale)
    dkv = jnp.concatenate([dk] + dvs, axis=1).astype(BF)
    dkv_ref[...] = dkv
    grad_ref[...] = dot_tn(dkv, x_ref[...]).astype(BF)
    put_slices(grad_ref, 0, sent_ref, kept_ref, info_ref[0] & 1)


def tokens_kernel(cols, dq_ref, dkv_ref, qo_ref, kv_ref, one_ref, out_ref):
    back = dot(dq_ref[...], qo_ref[:cols, :]) + dot(dkv_ref[...], kv_ref[...])

    @pl.when(pl.program_id(0) == 0)
    def _():
        out_ref[...] = one_ref[...] + back

    @pl.when(pl.program_id(0) > 0)
    def _():
        out_ref[...] += back


def norm_of(hidden):
    average = jnp.mean(hidden, axis=-1, keepdims=True)
    centred = hidden - average
    inverse = lax.rsqrt(jnp.mean(centred * centred, axis=-1, keepdims=True) + EPSILON)
    return centred * inverse, inverse


def norm_back(grad_in, normed, inverse, gain):
    scaled = grad_in * gain
    centred = (
        scaled
        - jnp.mean(scaled, axis=-1, keepdims=True)
        - normed * jnp.mean(scaled * normed, axis=-1, keepdims=True)
    )
    return centred * inverse


def column_sums(arrays, rows):
    sums = [jnp.sum(a, axis=0, keepdims=True) for a in arrays]
    return jnp.concatenate(sums + [jnp.zeros((rows - len(sums), sums[0].shape[1]), F32)], axis=0)


def gelu_both(v):
    t = 1.0 / (1.0 + (0.3275911 * 0.5**0.5) * jnp.abs(v))
    tail = 1.061405429 * 0.5
    for c in (-1.453152027, 1.421413741, -0.284496736, 0.254829592):
        tail = tail * t + 0.5 * c
    bell = jnp.exp(-0.5 * v * v)
    tail = tail * t * bell
    gate = jnp.where(v < 0.0, tail, 1.0 - tail)
    return v * gate, gate + v * bell * (2.0 * jnp.pi) ** (-0.5)


def ffn_kernel(
    first_ref, up_ref, down_ref, bup_ref, normed_ref, cot_ref, vec_ref,
    act_ref, slope_ref, out_ref, two_ref, low_ref, sums_ref, acc_ref,
):
    g = pl.program_id(0)
    act, slope = gelu_both(dot(first_ref[...], up_ref[...]) + bup_ref[...])
    act = act.astype(BF)
    act_ref[...] = act
    slope_ref[...] = slope.astype(BF)
    branch = dot(act, down_ref[...])

    @pl.when(g == 0)
    def _():
        acc_ref[...] = normed_ref[...] * vec_ref[0:1, :] + vec_ref[1:2, :] + vec_ref[2:3, :] + branch

    @pl.when(g > 0)
    def _():
        acc_ref[...] += branch

    @pl.when(g == pl.num_programs(0) - 1)
    def _():
        normed, inverse = norm_of(acc_ref[...])
        gain = vec_ref[3:4, :]
        out_ref[...] = (normed * gain + vec_ref[4:5, :]).astype(BF)
        grad_in = cot_ref[...].astype(F32)
        two = norm_back(grad_in, normed, inverse, gain)
        two_ref[...] = two
        low_ref[...] = two.astype(BF)
        sums_ref[...] = column_sums([grad_in * normed, grad_in, two], 8)


def ffn_back_kernel(
    info_ref, low_ref, act_ref, slope_ref, up_ref, down_ref, first_ref, two_ref, normed_ref, inverse_ref, vec_ref,
    sent_ref, kept_ref, bup_ref, one_ref, onelow_ref, sums_ref, acc_ref, grad_ref,
):
    g = pl.program_id(0)
    core = info_ref[0] & 1
    step = up_ref.shape[0] // PLANE
    low = low_ref[...]
    dpre = dot_nt(low, down_ref[...]) * slope_ref[...].astype(F32)
    bup_ref[...] = jnp.sum(dpre, axis=0, keepdims=True)
    pre_low = dpre.astype(BF)
    grad_ref[...] = dot_tn(first_ref[...], pre_low).astype(BF)
    put_slices(grad_ref, 0, sent_ref, kept_ref, core)
    grad_ref[...] = dot_tn(act_ref[...], low).astype(BF)
    put_slices(grad_ref, step, sent_ref, kept_ref, core)
    through = dot_nt(pre_low, up_ref[...])

    @pl.when(g == 0)
    def _():
        acc_ref[...] = two_ref[...] + through

    @pl.when(g > 0)
    def _():
        acc_ref[...] += through

    @pl.when(g == pl.num_programs(0) - 1)
    def _():
        grad_in = acc_ref[...]
        normed = normed_ref[...]
        one = norm_back(grad_in, normed, inverse_ref[:, 0:1], vec_ref[0:1, :])
        one_ref[...] = one
        onelow_ref[...] = one.astype(BF)
        sums_ref[...] = column_sums([grad_in * normed, grad_in, one], 8)


def body(
    rows, heads,
    tokens, segment_ids, w_qkv, b_qkv, w_out, b_out, gain_one, bias_one, w_up, b_up, w_down, b_down,
    gain_two, bias_two, omega, cotangent,
):
    rank = lax.axis_index("rows")
    level = lax.axis_index("heads")
    hd, feats = omega.shape
    _, length, width = tokens.shape
    cols = w_qkv.shape[2]
    nh = cols // hd
    hidden = w_up.shape[1]
    slots = plane_slots(rank)
    me = slots[0]
    info = jnp.stack(slots + [level]).astype(jnp.int32)
    x = tokens[0]

    def slice_of(array):
        step = array.shape[0] // PLANE
        return lax.dynamic_slice_in_dim(array, me * step, step, 0)

    def gather_weights(*owns):
        piece = jnp.concatenate([slice_of(own) for own in owns], axis=0)
        near = [permute(piece, "heads", heads, lambda i, m=m: i ^ m) for m in range(1, heads)]
        return place_weights(owns, plane_gather(jnp.stack(near), rows), info)

    wt = jnp.transpose(w_qkv, (1, 2, 0)).reshape(3 * cols, width)
    own_qo = jnp.concatenate([wt[:cols], w_out], axis=0)
    (kv_w,) = gather_weights(wt[cols:])
    biases = jnp.concatenate([b_qkv.reshape(-1), b_up])
    biases = to_heads(jnp.broadcast_to(biases[None, None], (heads, 1, biases.size)))
    (qo_w,) = gather_weights(own_qo)
    up_w, down_w = gather_weights(w_up, w_down)
    bias_q = biases[:, :, :cols]
    bias_kv = biases[:, :, cols : 3 * cols]
    bias_up = biases[:, :, 3 * cols :]

    segments = lax.dynamic_slice_in_dim(segment_ids[0], level * length, length, 0)
    by_level = segment_ids[0].reshape(heads, length)
    firsts, lasts = by_level[:, 0], by_level[:, -1]
    my_first, my_last = segments[0], segments[-1]
    ends = jnp.stack([segments == my_first, segments == my_last], axis=1).astype(F32)
    same = (segments[:, None] == segments[None, :]).astype(BF)
    index = jnp.arange(heads)
    match = jnp.concatenate(
        [(index < level) & (lasts == my_first), (index > level) & (firsts == my_last)]
    ).astype(F32)

    eye = jnp.eye(nh, dtype=BF)
    om = (eye[:, None, :, None] * omega[None, :, None, :]).reshape(cols, nh * feats)
    edge = cols + 16
    dims = (nh, hd, feats)
    t = length
    aug = width + 128
    ones = jnp.ones((t, 1), BF)
    blank = jnp.zeros((t, 127), BF)
    x_aug = jnp.concatenate([x, ones, blank], axis=1)
    edge_spec = pl.BlockSpec((heads, None, edge, feats), lambda g: (0, g, 0, 0))
    half = PLANE // 2

    kv, phi_k, edges = call(
        functools.partial(keys_kernel, *dims),
        (heads,),
        [
            SMEM_SPEC, whole(t, width), part(2 * cols, width), part(1, 2 * cols), whole(cols, nh * feats),
            whole(t, 2),
        ],
        [part(t, 2 * cols), part(t, nh * feats), edge_spec],
        [
            struct((heads, t, 2 * cols), BF),
            struct((heads, t, nh * feats), BF),
            struct((heads, heads, edge, feats), BF),
        ],
        (info, x, kv_w, bias_kv, om, ends),
        us=12,
    )
    came = to_heads(edges)
    q, phi_q, near = call(
        functools.partial(queries_kernel, *dims),
        (heads,),
        [
            whole(t, width), part(2 * cols, width), part(1, cols), whole(cols, nh * feats), whole(t, t),
            part(t, 2 * cols), part(t, nh * feats),
        ],
        [part(t, cols), part(t, nh * feats), part(t, 2 * cols)],
        [
            struct((heads, t, cols), BF),
            struct((heads, t, nh * feats), BF),
            struct((heads, t, 2 * cols), F32),
        ],
        (x, qo_w, bias_q, om, same, kv, phi_k),
        us=12,
    )
    vec_one = jnp.stack([gain_one, bias_one])
    att, den, far_f, far_l, normed_one, inverse_one, first_low = call(
        functools.partial(attend_kernel, *dims),
        (heads,),
        [
            SMEM_SPEC, part(t, nh * feats), part(t, 2 * cols), edge_spec, whole(t, 2), part(2 * cols, width),
            whole(t, width), whole(1, width), whole(2, width),
        ],
        [
            part(t, cols), part(t, 128), part(edge, feats), part(edge, feats), whole(t, width), whole(t, 128),
            whole(t, width),
        ],
        [
            struct((heads, t, cols), BF),
            struct((heads, t, 128), F32),
            struct((heads, edge, feats), BF),
            struct((heads, edge, feats), BF),
            struct((t, width), F32),
            struct((t, 128), F32),
            struct((t, width), BF),
        ],
        (match, phi_q, near, came, ends, qo_w, x, b_out[None], vec_one),
        us=10,
        scratch=[pltpu.VMEM((t, width), F32)],
    )

    vec_two = jnp.stack([gain_one, bias_one, b_down, gain_two, bias_two])
    act, slope, layer_output, grad_two, two_low, sums_two = call(
        ffn_kernel,
        (heads,),
        [
            whole(t, width), part(width, hidden), part(hidden, width), part(1, hidden), whole(t, width),
            whole(t, width), whole(5, width),
        ],
        [part(t, hidden), part(t, hidden), whole(t, width), whole(t, width), whole(t, width), whole(8, width)],
        [
            struct((heads, t, hidden), BF),
            struct((heads, t, hidden), BF),
            struct((t, width), BF),
            struct((t, width), F32),
            struct((t, width), BF),
            struct((8, width), F32),
        ],
        (first_low, up_w, down_w, bias_up, normed_one, cotangent[0], vec_two),
        us=12,
        scratch=[pltpu.VMEM((t, width), F32)],
    )
    step = width // PLANE
    ffn_sent, ffn_kept, grad_b_up, grad_one, one_low, sums_one = call(
        ffn_back_kernel,
        (heads,),
        [
            SMEM_SPEC, whole(t, width), part(t, hidden), part(t, hidden), part(width, hidden), part(hidden, width),
            whole(t, width), whole(t, width), whole(t, width), whole(t, 128), whole(2, width),
        ],
        [
            part(half, 2 * step, width), part(half, 2 * step, width), part(1, hidden), whole(t, width),
            whole(t, width), whole(8, width),
        ],
        [
            struct((heads, half, 2 * step, width), BF),
            struct((heads, half, 2 * step, width), BF),
            struct((heads, 1, hidden), F32),
            struct((t, width), F32),
            struct((t, width), BF),
            struct((8, width), F32),
        ],
        (info, two_low, act, slope, up_w, down_w, first_low, grad_two, normed_one, inverse_one, vec_one),
        us=16,
        scratch=[pltpu.VMEM((t, width), F32), pltpu.VMEM((width, hidden), BF)],
    )
    ffn_pieces = reduce_grads(ffn_sent, ffn_kept, rank, rows)

    dnd, edges = call(
        functools.partial(attend_back_kernel, *dims),
        (heads,),
        [
            SMEM_SPEC, whole(t, width), part(2 * cols, width), part(t, cols), part(t, 128), part(t, nh * feats),
            whole(t, 2),
        ],
        [part(t, 2 * cols), edge_spec],
        [struct((heads, t, 2 * cols), BF), struct((heads, heads, edge, feats), BF)],
        (info, one_low, qo_w, att, den, phi_q, ends),
        us=13,
    )
    back = to_heads(edges)
    one_aug = jnp.concatenate([one_low, ones, blank], axis=1)
    slice_rows = 2 * cols // PLANE
    dq, dphi_k, dv, qo_sent, qo_kept = call(
        functools.partial(queries_back_kernel, *dims),
        (heads,),
        [
            SMEM_SPEC, part(t, 2 * cols), part(t, cols), part(t, nh * feats), part(t, 2 * cols),
            part(t, nh * feats), part(edge, feats), part(edge, feats), whole(cols, nh * feats), whole(t, t),
            whole(t, 2), part(t, cols), whole(t, aug), whole(t, aug),
        ],
        [
            part(t, cols), part(t, nh * feats), part(t, cols), part(half, slice_rows, aug),
            part(half, slice_rows, aug),
        ],
        [
            struct((heads, t, cols), BF),
            struct((heads, t, nh * feats), F32),
            struct((heads, t, cols), F32),
            struct((heads, half, slice_rows, aug), BF),
            struct((heads, half, slice_rows, aug), BF),
        ],
        (info, dnd, q, phi_q, kv, phi_k, far_f, far_l, om, same, ends, att, x_aug, one_aug),
        us=20,
        scratch=[pltpu.VMEM((2 * cols, aug), BF)],
    )
    qo_pieces = reduce_grads(qo_sent, qo_kept, rank, rows)
    dkv, kv_sent, kv_kept = call(
        functools.partial(keys_back_kernel, *dims),
        (heads,),
        [
            SMEM_SPEC, SMEM_SPEC, part(t, 2 * cols), part(t, nh * feats), part(t, nh * feats), part(t, cols),
            edge_spec, whole(cols, nh * feats), whole(t, 2), whole(t, aug),
        ],
        [part(t, 2 * cols), part(half, slice_rows, aug), part(half, slice_rows, aug)],
        [
            struct((heads, t, 2 * cols), BF),
            struct((heads, half, slice_rows, aug), BF),
            struct((heads, half, slice_rows, aug), BF),
        ],
        (info, match, kv, phi_k, dphi_k, dv, back, om, ends, x_aug),
        us=12,
        scratch=[pltpu.VMEM((2 * cols, aug), BF)],
    )
    kv_pieces = reduce_grads(kv_sent, kv_kept, rank, rows)
    grad_tokens = call(
        functools.partial(tokens_kernel, cols),
        (heads,),
        [part(t, cols), part(t, 2 * cols), part(2 * cols, width), part(2 * cols, width), whole(t, width)],
        whole(t, width),
        struct((t, width), F32),
        (dq, dkv, qo_w, kv_w, grad_one),
        us=5,
    )

    shared = jnp.concatenate([sums_one[:3], sums_two[:3]], axis=0).reshape(1, 6 * width)
    shared = jnp.broadcast_to(shared, (heads, 6 * width))
    vectors = jnp.concatenate([shared, grad_b_up[:, 0]], axis=1)
    vectors = lax.all_to_all(
        jnp.broadcast_to(vectors[None], (rows, *vectors.shape)), "rows", 0, 0, tiled=True
    )
    vectors = jnp.sum(vectors, axis=0)
    vectors = jnp.sum(to_heads(vectors[:, None, :]), axis=0)[0]
    outs = [vectors[n * width : (n + 1) * width] for n in range(6)]
    out_b_up = vectors[6 * width :]

    out_up, out_down = place_ffn(ffn_pieces, info)
    out_qkv, out_o, out_b = place_attention(qo_pieces, kv_pieces, info, cols, width)
    out_qkv = jnp.transpose(out_qkv.reshape(3, cols, width), (2, 0, 1))
    return (
        layer_output[None],
        grad_tokens[None],
        out_qkv,
        out_b[:, 0].reshape(3, cols),
        out_o,
        outs[2],
        outs[0],
        outs[1],
        out_up,
        out_b_up,
        out_down,
        outs[5],
        outs[3],
        outs[4],
    )


def solution(mesh):
    return jax.shard_map(
        functools.partial(body, mesh.shape["rows"], mesh.shape["heads"]),
        mesh=mesh,
        in_specs=(
            P("rows", "heads", None),
            P("rows", None),
            P(None, None, "heads"),
            P(None, "heads"),
            P("heads", None),
            P(),
            P(),
            P(),
            P(None, "heads"),
            P("heads"),
            P("heads", None),
            P(),
            P(),
            P(),
            P(),
            P("rows", "heads", None),
        ),
        out_specs=(
            P("rows", "heads", None),
            P("rows", "heads", None),
            P(None, None, "heads"),
            P(None, "heads"),
            P("heads", None),
            P(),
            P(),
            P(),
            P(None, "heads"),
            P("heads"),
            P("heads", None),
            P(),
            P(),
            P(),
        ),
        check_vma=False,
    )
```

time: 888 us -> 423 us (0.48)
  waiting for transfers between devices: 649 us -> 118 us
  Pallas kernels: 0 us -> 144 us
  matrix products: 115 us -> 0 us
  starting transfers between devices: 1.2 us -> 82.2 us
  blocking collectives: 44 us -> 0 us
  between operations: 15 us -> 1.93 us
  local copies, waits for them, and re-layouts: 20.7 us -> 33.7 us
    reduce_scatter x4 -> x0, waiting for transfers between devices: 278 us -> none  [the longest x1 110 us: body(): lax.psum_scatter(first_terms, 'heads', scatter_dimension=1, tiled=True)]
    all_gather x4 -> x0, waiting for transfers between devices: 258 us -> none  [the longest x1 67.1 us: body(): full_tokens = lax.all_gather(tokens, 'heads', axis=1, tiled=True)]
    pallas_call x0 -> x14, Pallas kernels: none -> 144 us  [the longest x9 125 us: call(): pl.pallas_call(kernel, grid=grid, in_specs=in_specs, out_specs=out_specs,...]
    psum x1 -> x0, waiting for transfers between devices: 112 us -> none  [body(): lax.psum((grad_w_qkv, grad_b_qkv, grad_w_out, grad_w_up, grad_b_up, grad_...]
    dot_general x25 -> x0, matrix products: 111 us -> none  [the longest x1 18.4 us: body(): jnp.einsum('rld,df->rlf', full_first, w_up, preferred_element_type=jnp.fl...]
    ppermute x0 -> x60, waiting for transfers between devices: none -> 78.3 us  [permute(): return lax.ppermute(array, axis, [(i, partner(i)) for i in range(size)])]
    ppermute x0 -> x60, starting transfers between devices: none -> 50.8 us  [permute(): return lax.ppermute(array, axis, [(i, partner(i)) for i in range(size)])]
    psum x2 -> x0, blocking collectives: 44 us -> none  [the longest x1 23.8 us: body(): lax.psum((grad_w_qkv, grad_b_qkv, grad_w_out, grad_w_up, grad_b_up, grad_...]
  transfers between devices with their start and end apart: 9 -> 68, of which waited for: 8 -> 19; matrix products, arithmetic and copies ran while one was open for 2% -> 11% of each run, Pallas kernels for 0% -> 23%
where the time goes in v1:
time: 423 us; the launch traced here: 417 us
  Pallas kernels  144 us (34%)
  waiting for transfers between devices  118 us (28%)
  starting transfers between devices  82.2 us (19%)
  other arithmetic  36.1 us (9%)
  local copies, waits for them, and re-layouts  33.7 us (8%)
    pallas_call x9, Pallas kernels, call(): pl.pallas_call(kernel, grid=grid, in_specs=in_specs, out_specs=out_specs,...  125 us
    ppermute x60, waiting for transfers between devices, permute(): return lax.ppermute(array, axis, [(i, partner(i)) for i in range(size)])  78.3 us
    ppermute x60, starting transfers between devices, permute(): return lax.ppermute(array, axis, [(i, partner(i)) for i in range(size)])  50.8 us
    all_to_all x7, starting transfers between devices, to_heads(): return lax.all_to_all(array, 'heads', 0, 0, tiled=True)  27.9 us
    all_to_all x7, waiting for transfers between devices, to_heads(): return lax.all_to_all(array, 'heads', 0, 0, tiled=True)  24.5 us
    unnamed x93, local copies, waits for them, and re-layouts  16.4 us
    all_to_all x1, waiting for transfers between devices, body(): lax.all_to_all(jnp.broadcast_to(vectors[None], (rows, *vectors.shape)), '...  15.6 us
    pallas_call x3, Pallas kernels, place_weights(): pl.pallas_call(functools.partial(place_weights_kernel, count, parts), gri...  13.8 us
  transfers between devices with their start and end apart: 68, of which 19 were waited for; matrix products, arithmetic and copies ran while one was open for 11% of the time, Pallas kernels for 23%

profile of v1, /device:TPU:0, one launch (start us, length us, event | category | flops | bytes accessed | tf_op | source)
XLA Modules:
  0.0 416.9 jit_solution(10099921631580794811)
XLA Ops:
  2.5 3.0 collective-permute-start.20
  5.6 2.6 collective-permute-start.21
  9.2 3.5 collective-permute-start.11
  13.4 3.3 all-to-all-start
  20.7 6.6 %collective-permute-done.10 = bf16[48,768]{1,0:T(8,128)(2,1)S(1)} collective-permute-done((bf16[48,768]{1,0:T(8,128)(2,1)S(1)}, bf16[48,768]{1,0:T(8,128)(2,1)S(1)}, u32[]{:S(2)}, u32[]{:S(2)}) %collective-permute-start.10) | collective-permute-done | bytes 73760 | tf_op jit(solution)/shard_map/ppermute | solution.py:59
  27.3 2.6 collective-permute-start.12
  30.0 10.1 %collective-permute-done.11 = bf16[48,768]{1,0:T(8,128)(2,1)S(1)} collective-permute-done((bf16[48,768]{1,0:T(8,128)(2,1)S(1)}, bf16[48,768]{1,0:T(8,128)(2,1)S(1)}, u32[]{:S(2)}, u32[]{:S(2)}) %collective-permute-start.11) | collective-permute-done | bytes 73760 | tf_op jit(solution)/shard_map/ppermute | solution.py:59
  40.1 3.1 collective-permute-start.1
  45.4 1.5 collective-permute-start.13
  50.2 1.5 collective-permute-start.14
  51.7 1.6 collective-permute-done.13.refs_2_
  53.4 1.5 collective-permute-start.15
  56.3 1.6 collective-permute-start.3
  59.9 3.5 collective-permute-done.15.refs_4_
  64.6 3.6 collective-permute-done.3.refs_2_
  68.2 1.5 collective-permute-start.4
  70.3 1.5 collective-permute-start.5
  72.7 3.1 shard_map.264.w_ref.kv_ref
  77.7 12.9 %shard_map.265 = (bf16[4,512,384]{2,1,0:T(8,128)(2,1)S(1)}, bf16[4,512,768]{2,1,0:T(8,128)(2,1)}, bf16[4,4,208,256]{3,2,1,0:T(8,128)(2,1)}) custom-call(s32[9]{0:T(128)S(1)} %stack.121.info_ref, bf16[512,768]{1,0:T(8,128)(2,1)S(1)} %bitcast.117, bf16[4,384,768]{2,1,0:T(8,128)(2,1)} %copy-done.9, f32[4,1,384]{2,1,0:T(1,128)S(1)} %slice.143.b_ref, ...), custom_call_target="tpu_custom_call" | custom-call | flops 13200000000 | tf_op jit(solution)/shard_map/pallas_call | solution.py:34
  91.8 4.7 %all-to-all-start.1 = ((bf16[4,4,208,256]{3,2,1,0:T(8,128)(2,1)}), bf16[4,4,208,256]{3,2,1,0:T(8,128)(2,1)}, u32[]{:S(2)}, u32[]{:S(2)}) async-start(bf16[4,4,208,256]{3,2,1,0:T(8,128)(2,1)} %get-tuple-element.60), calls=%async_computation.1 | async-start | bytes 3407872 | tf_op jit(solution)/shard_map/all_to_all | solution.py:101
  100.3 2.8 shard_map.263.w_ref.qo_ref
  105.4 12.0 %shard_map.266 = (bf16[4,512,192]{2,1,0:T(8,128)(2,1)S(1)}, bf16[4,512,768]{2,1,0:T(8,128)(2,1)}, f32[4,512,384]{2,1,0:T(8,128)}) custom-call(bf16[512,768]{1,0:T(8,128)(2,1)S(1)} %bitcast.118, bf16[4,384,768]{2,1,0:T(8,128)(2,1)} %copy-done.10, f32[4,1,192]{2,1,0:T(1,128)S(1)} %slice.141.b_ref, bf16[192,768]{1,0:T(8,128)(2,1)S(1)} %bitcast.124, ...), custom_call_target="tpu_custom_call" | custom-call | flops 13200000000 | tf_op jit(solution)/shard_map/pallas_call | solution.py:34
  119.3 7.9 %shard_map.268 = (bf16[4,768,768]{2,1,0:T(8,128)(2,1)}, bf16[4,768,768]{2,1,0:T(8,128)(2,1)}) custom-call(s32[9]{0:T(128)S(1)} %stack.121.info_ref, bf16[768,768]{1,0:T(8,128)(2,1)} %refs_0_.1, bf16[768,768]{1,0:T(8,128)(2,1)} %refs_1_.1, bf16[3,192,768]{2,1,0:T(8,128)(2,1)S(1)} %pad_maximum_fusion.1.refs_2_, ...), custom_call_target="tpu_custom_call" | custom-call | flops 6600000000 | tf_op jit(solution)/shard_map/pallas_call | solution.py:163
  127.2 10.1 %all-to-all-done.1.came_ref = bf16[4,4,208,256]{3,2,1,0:T(8,128)(2,1)} async-done(((bf16[4,4,208,256]{3,2,1,0:T(8,128)(2,1)}), bf16[4,4,208,256]{3,2,1,0:T(8,128)(2,1)}, u32[]{:S(2)}, u32[]{:S(2)}) %all-to-all-start.1) | async-done | bytes 1703968 | tf_op jit(solution)/shard_map/all_to_all | solution.py:101
  137.3 11.6 %shard_map.267 = (bf16[4,512,192]{2,1,0:T(8,128)(2,1)S(1)}, f32[4,512,128]{2,1,0:T(8,128)S(1)}, bf16[4,208,256]{2,1,0:T(8,128)(2,1)S(1)}, bf16[4,208,256]{2,1,0:...) custom-call(f32[8]{0:T(128)S(1)} %add_convert_fusion.6.match_ref, ...), custom_call_target="tpu_custom_call" | custom-call | flops 11000000512 | tf_op jit(solution)/shard_map/pallas_call | solution.py:34
  149.0 1.8 copy-done.17
  150.7 14.9 %shard_map.269 = (bf16[4,512,768]{2,1,0:T(8,128)(2,1)}, bf16[4,512,768]{2,1,0:T(8,128)(2,1)}, bf16[512,768]{1,0:T(8,128)(2,1)}, f32[512,768]{1,0:T(8,128)S(1)}, ...) custom-call(bf16[512,768]{1,0:T(8,128)(2,1)S(1)} %get-tuple-element.61.first_ref, ...), custom_call_target="tpu_custom_call" | custom-call | flops 13200000000 | tf_op jit(solution)/shard_map/pallas_call | solution.py:34
  165.6 19.0 %shard_map.270 = (bf16[4,4,192,768]{3,2,1,0:T(8,128)(2,1)}, bf16[4,4,192,768]{3,2,1,0:T(8,128)(2,1)}, f32[4,1,768]{2,1,0:T(1,128)S(1)}, f32[512,768]{1,0:T(8,128...) custom-call(s32[9]{0:T(128)S(1)} %stack.121.info_ref, bf16[512,768]{1,0:T(8,128)(2,1)S(1)} %get-tuple-element.66.low_ref, ...), custom_call_target="tpu_custom_call" | custom-call | flops 17600000000 | tf_op jit(solution)/shard_map/pallas_call | solution.py:34
  184.7 5.5 %copy.119 = bf16[4,4,192,768]{3,2,0,1:T(8,128)(2,1)} copy(bf16[4,4,192,768]{3,2,1,0:T(8,128)(2,1)} %get-tuple-element.95) | data formatting | bytes 9437184 | tf_op jit(solution)/shard_map/pallas_call | solution.py:34
  191.2 14.9 %shard_map.271 = (bf16[4,512,384]{2,1,0:T(8,128)(2,1)S(1)}, bf16[4,4,208,256]{3,2,1,0:T(8,128)(2,1)}) custom-call(s32[9]{0:T(128)S(1)} %stack.121.info_ref, bf16[512,768]{1,0:T(8,128)(2,1)S(1)} %get-tuple-element.71.dh_ref, bf16[4,384,768]{2,1,0:T(8,128)(2,1)} %copy-done.10, bf16[4,512,192]{2,1,0:T(8,128)(2,1)S(1)} %get-tuple-element.72.att_ref, ...), custom_call_target="tpu_custom_call" | custom-call | flops 14300000256 | tf_op jit(solution)/shard_map/pallas_call | solution.py:34
  207.3 20.8 %shard_map.272 = (bf16[4,512,192]{2,1,0:T(8,128)(2,1)S(1)}, f32[4,512,768]{2,1,0:T(8,128)}, f32[4,512,192]{2,1,0:T(8,128)}, bf16[4,4,48,896]{3,2,1,0:T(8,128)(2,1)}, bf16[4,4,48,896]{3,2,1,0:T(8,128)(2,1)}) custom-call(s32[9]{0:T(128)S(1)} %stack.121.info_ref, bf16[4,512,384]{2,1,0:T(8,128)(2,1)} %copy-done.21, bf16[4,512,192]{2,1,0:T(8,128)(2,1)S(1)} %copy-done.23, ...), custom_call_target="tpu_custom_call" | custom-call | flops 22000001024 | tf_op jit(solution)/shard_map/pallas_call | solution.py:34
  228.1 2.9 copy.107
  231.5 4.6 %all-to-all-start.2 = ((bf16[4,4,208,256]{3,2,1,0:T(8,128)(2,1)}), bf16[4,4,208,256]{3,2,1,0:T(8,128)(2,1)}, u32[]{:S(2)}, u32[]{:S(2)}) async-start(bf16[4,4,208,256]{3,2,1,0:T(8,128)(2,1)} %get-tuple-element.81), calls=%async_computation.2 | async-start | bytes 3407872 | tf_op jit(solution)/shard_map/all_to_all | solution.py:101
  236.2 2.9 fusion.4
  239.1 1.6 pad_maximum_fusion
  243.5 1.5 collective-permute-start.31
  245.1 32.1 %collective-permute-done.31 = bf16[2,4,48,896]{3,2,1,0:T(8,128)(2,1)S(1)} collective-permute-done((bf16[2,4,48,896]{3,2,1,0:T(8,128)(2,1)}, bf16[2,4,48,896]{3,2,1,0:T(8,128)(2,1)S(1)}, u32[]{:S(2)}, u32[]{:S(2)}) %collective-permute-start.31) | collective-permute-done | bytes 688160 | tf_op jit(solution)/shard_map/ppermute | solution.py:59
  277.2 2.2 fusion.10
  279.9 12.9 %shard_map.273 = (bf16[4,512,384]{2,1,0:T(8,128)(2,1)S(1)}, bf16[4,4,48,896]{3,2,1,0:T(8,128)(2,1)S(1)}, bf16[4,4,48,896]{3,2,1,0:T(8,128)(2,1)S(1)}) custom-call(s32[9]{0:T(128)S(1)} %stack.121.info_ref, f32[8]{0:T(128)S(1)} %add_convert_fusion.6.match_ref, bf16[4,512,384]{2,1,0:T(8,128)(2,1)} %copy-done.18, ...), custom_call_target="tpu_custom_call" | custom-call | flops 13200000000 | tf_op jit(solution)/shard_map/pallas_call | solution.py:34
  294.2 3.4 fusion
  300.1 3.5 all-to-all-start.5
  303.6 2.1 fusion.13
  305.7 15.6 %all-to-all-done.5 = f32[8,4,5376]{2,1,0:T(4,128)S(1)} async-done(((f32[8,4,5376]{2,1,0:T(4,128)}), f32[8,4,5376]{2,1,0:T(4,128)S(1)}, u32[]{:S(2)}, u32[]{:S(2)}) %all-to-all-start.5) | async-done | bytes 688160 | tf_op jit(solution)/shard_map/all_to_all | solution.py:817
  321.3 5.1 %all-to-all-start.3 = ((bf16[4,48,896]{2,1,0:T(8,128)(2,1)}), bf16[4,48,896]{2,1,0:T(8,128)(2,1)S(1)}, u32[]{:S(2)}, u32[]{:S(2)}) async-start(bf16[4,48,896]{2,1,0:T(8,128)(2,1)} %fusion.13), calls=%async_computation.3 | async-start | bytes 688128 | tf_op jit(solution)/shard_map/all_to_all | solution.py:101
  326.4 3.9 fusion.3
  330.3 5.6 %all-to-all-done.3 = bf16[4,48,896]{2,1,0:T(8,128)(2,1)S(1)} async-done(((bf16[4,48,896]{2,1,0:T(8,128)(2,1)}), bf16[4,48,896]{2,1,0:T(8,128)(2,1)S(1)}, u32[]{:S(2)}, u32[]{:S(2)}) %all-to-all-start.3) | async-done | bytes 344096 | tf_op jit(solution)/shard_map/all_to_all | solution.py:101
  336.7 3.5 all-to-all-start.7
  342.4 10.2 %collective-permute-done.41 = bf16[2,4,48,896]{3,2,1,0:T(8,128)(2,1)S(1)} collective-permute-done((bf16[2,4,48,896]{3,2,1,0:T(8,128)(2,1)S(1)}, bf16[2,4,48,896]{3,2,1,0:T(8,128)(2,1)S(1)}, u32[]{:S(2)}, u32[]{:S(2)}) %collective-permute-start.41) | collective-permute-done | bytes 688160 | tf_op jit(solution)/shard_map/ppermute | solution.py:59
  353.7 2.5 collective-permute-start.42
  356.3 5.2 %collective-permute-done.42 = bf16[4,48,896]{2,1,0:T(8,128)(2,1)S(1)} collective-permute-done((bf16[4,48,896]{2,1,0:T(8,128)(2,1)S(1)}, bf16[4,48,896]{2,1,0:T(8,128)(2,1)S(1)}, u32[]{:S(2)}, u32[]{:S(2)}) %collective-permute-start.42) | collective-permute-done | bytes 344096 | tf_op jit(solution)/shard_map/ppermute | solution.py:59
  361.5 1.9 fusion.9
  363.4 3.6 all-to-all-done.7
  368.0 3.5 all-to-all-start.4
  371.4 1.6 reduce_sum.61.refs_0_
  373.1 2.6 collective-permute-start.53
  377.8 3.7 all-to-all-done.4
  381.5 3.3 all-to-all-start.6
  386.7 2.4 collective-permute-start.43
  391.4 2.2 collective-permute-start.46
  395.5 2.5 collective-permute-done.45.refs_11_
  398.0 2.0 collective-permute-start.55
  402.9 6.5 %shard_map.274 = f32[512,768]{1,0:T(8,128)} custom-call(bf16[4,512,192]{2,1,0:T(8,128)(2,1)S(1)} %copy-done.16, bf16[4,512,384]{2,1,0:T(8,128)(2,1)S(1)} %copy-done.14, bf16[4,384,768]{2,1,0:T(8,128)(2,1)} %copy-done.10, bf16[4,384,768]{2,1,0:T(8,128)(2,1)} %copy-done.9, f32[512,768]{1,0:T(8,128)S(1)} %copy-done.12), custom_call_target="tpu_custom_call" | custom-call | flops 5500000256 | tf_op jit(solution)/shard_map/pallas_call | solution.py:34
  410.4 2.2 shard_map.275
  413.4 3.0 shard_map.276
  (254 shorter events, 57.9 us)
Async XLA Ops:
  2.5 41.5 %collective-permute-start.20 = (bf16[192,768]{1,0:T(8,128)(2,1)}, bf16[192,768]{1,0:T(8,128)(2,1)S(1)}, u32[]{:S(2)}, u32[]{:S(2)}) collective-permute-start(bf16[192,768]{1,0:T(8,128)(2,1)} %pad_maximum_fusion.5), channel_id=1, source_target_pairs={{0,1},{1,0},{2,3},{3,2},{4,5},{5,4},{6,7},{7,6},{8,9},{9,8},{10,11... | collective-permute-start | bytes 884744 | tf_op jit(solution)/shard_map/ppermute | solution.py:59
  5.6 39.9 %collective-permute-start.21 = (bf16[192,768]{1,0:T(8,128)(2,1)}, bf16[192,768]{1,0:T(8,128)(2,1)S(1)}, u32[]{:S(2)}, u32[]{:S(2)}) collective-permute-start(bf16[192,768]{1,0:T(8,128)(2,1)} %pad_maximum_fusion.5), channel_id=1, source_target_pairs={{0,2},{1,3},{2,0},{3,1},{4,6},{5,7},{6,4},{7,5},{8,10},{9,11},{10,... | collective-permute-start | bytes 884744 | tf_op jit(solution)/shard_map/ppermute | solution.py:59
  8.1 38.8 %collective-permute-start.22 = (bf16[192,768]{1,0:T(8,128)(2,1)}, bf16[192,768]{1,0:T(8,128)(2,1)}, u32[]{:S(2)}, u32[]{:S(2)}) collective-permute-start(bf16[192,768]{1,0:T(8,128)(2,1)} %pad_maximum_fusion.5), channel_id=1, source_target_pairs={{0,3},{1,2},{2,1},{3,0},{4,7},{5,6},{6,5},{7,4},{8,11},{9,10},{10,... | collective-permute-start | bytes 884744 | tf_op jit(solution)/shard_map/ppermute | solution.py:59
  8.2 19.1 %collective-permute-start.10 = (bf16[48,768]{1,0:T(8,128)(2,1)S(1)}, bf16[48,768]{1,0:T(8,128)(2,1)S(1)}, u32[]{:S(2)}, u32[]{:S(2)}) collective-permute-start(bf16[48,768]{1,0:T(8,128)(2,1)S(1)} %constant_dynamic-slice_fusion.4), channel_id=1, source_target_pairs={{0,1},{1,0},{2,3},{3,2},{4,5},{5,4},{6,7},{7,6},{8,9},{9,8},{10,11... | collective-permute-start | bytes 221192 | tf_op jit(solution)/shard_map/ppermute | solution.py:59
  9.2 30.9 %collective-permute-start.11 = (bf16[48,768]{1,0:T(8,128)(2,1)S(1)}, bf16[48,768]{1,0:T(8,128)(2,1)S(1)}, u32[]{:S(2)}, u32[]{:S(2)}) collective-permute-start(bf16[48,768]{1,0:T(8,128)(2,1)S(1)} %constant_dynamic-slice_fusion.4), channel_id=1, source_target_pairs={{0,2},{1,3},{2,0},{3,1},{4,6},{5,7},{6,4},{7,5},{8,10},{9,11},{10,... | collective-permute-start | bytes 221192 | tf_op jit(solution)/shard_map/ppermute | solution.py:59
  13.4 51.1 %all-to-all-start = ((f32[4,1,1344]{2,1,0:T(1,128)}), f32[4,1,1344]{2,1,0:T(1,128)S(1)}, u32[]{:S(2)}, u32[]{:S(2)}) async-start(f32[4,1,1344]{2,1,0:T(1,128)} %broadcast_in_dim.20), calls=%async_computation | async-start | bytes 45056 | tf_op jit(solution)/shard_map/all_to_all | solution.py:101
  27.3 12.7 %collective-permute-start.12 = (bf16[48,768]{1,0:T(8,128)(2,1)S(1)}, bf16[48,768]{1,0:T(8,128)(2,1)S(1)}, u32[]{:S(2)}, u32[]{:S(2)}) collective-permute-start(bf16[48,768]{1,0:T(8,128)(2,1)S(1)} %constant_dynamic-slice_fusion.4), channel_id=1, source_target_pairs={{0,3},{1,2},{2,1},{3,0},{4,7},{5,6},{6,5},{7,4},{8,11},{9,10},{10,... | collective-permute-start | bytes 221192 | tf_op jit(solution)/shard_map/ppermute | solution.py:59
  40.0 10.1 %collective-permute-start = (bf16[48,768]{1,0:T(8,128)(2,1)S(1)}, bf16[48,768]{1,0:T(8,128)(2,1)S(1)}, u32[]{:S(2)}, u32[]{:S(2)}) collective-permute-start(bf16[48,768]{1,0:T(8,128)(2,1)S(1)} %fusion.18), channel_id=1, source_target_pairs={{0,1},{1,0},{2,3},{3,2},{4,5},{5,4},{6,7},{7,6},{8,9},{9,8},{10,11... | collective-permute-start | bytes 221192 | tf_op jit(solution)/shard_map/ppermute | solution.py:59
  40.1 11.7 %collective-permute-start.1 = (bf16[48,768]{1,0:T(8,128)(2,1)S(1)}, bf16[48,768]{1,0:T(8,128)(2,1)S(1)}, u32[]{:S(2)}, u32[]{:S(2)}) collective-permute-start(bf16[48,768]{1,0:T(8,128)(2,1)S(1)} %fusion.18), channel_id=1, source_target_pairs={{0,2},{1,3},{2,0},{3,1},{4,6},{5,7},{6,4},{7,5},{8,10},{9,11},{10,... | collective-permute-start | bytes 221192 | tf_op jit(solution)/shard_map/ppermute | solution.py:59
  44.0 12.2 %collective-permute-start.2 = (bf16[48,768]{1,0:T(8,128)(2,1)S(1)}, bf16[48,768]{1,0:T(8,128)(2,1)S(1)}, u32[]{:S(2)}, u32[]{:S(2)}) collective-permute-start(bf16[48,768]{1,0:T(8,128)(2,1)S(1)} %fusion.18), channel_id=1, source_target_pairs={{0,3},{1,2},{2,1},{3,0},{4,7},{5,6},{6,5},{7,4},{8,11},{9,10},{10,... | collective-permute-start | bytes 221192 | tf_op jit(solution)/shard_map/ppermute | solution.py:59
  45.4 7.9 %collective-permute-start.13 = (bf16[3,48,768]{2,1,0:T(8,128)(2,1)S(1)}, bf16[3,48,768]{2,1,0:T(8,128)(2,1)}, u32[]{:S(2)}, u32[]{:S(2)}) collective-permute-start(bf16[3,48,768]{2,1,0:T(8,128)(2,1)S(1)} %pad_maximum_fusion.7.refs_1_), channel_id=1, source_target_pairs={{0,8},{4,20},{8,0},{12,28},{16,24},{20,4},{24,16},{28,12},{1,9},{5... | collective-permute-start | bytes 663560 | tf_op jit(solution)/shard_map/ppermute | solution.py:59
  48.0 29.2 %collective-permute-start.23 = (bf16[3,192,768]{2,1,0:T(8,128)(2,1)S(1)}, bf16[3,192,768]{2,1,0:T(8,128)(2,1)}, u32[]{:S(2)}, u32[]{:S(2)}) collective-permute-start(bf16[3,192,768]{2,1,0:T(8,128)(2,1)S(1)} %pad_maximum_fusion.1.refs_2_), channel_id=1, source_target_pairs={{0,8},{4,20},{8,0},{12,28},{16,24},{20,4},{24,16},{28,12},{1,9},{5... | collective-permute-start | bytes 2654216 | tf_op jit(solution)/shard_map/ppermute | solution.py:59
  50.2 8.5 %collective-permute-start.14 = (bf16[3,48,768]{2,1,0:T(8,128)(2,1)S(1)}, bf16[3,48,768]{2,1,0:T(8,128)(2,1)}, u32[]{:S(2)}, u32[]{:S(2)}) collective-permute-start(bf16[3,48,768]{2,1,0:T(8,128)(2,1)S(1)} %pad_maximum_fusion.7.refs_1_), channel_id=1, source_target_pairs={{0,16},{4,12},{8,24},{12,4},{16,0},{20,28},{24,8},{28,20},{1,17},{... | collective-permute-start | bytes 663560 | tf_op jit(solution)/shard_map/ppermute | solution.py:59
  51.7 7.0 %collective-permute-start.16 = (bf16[3,48,768]{2,1,0:T(8,128)(2,1)S(1)}, bf16[3,48,768]{2,1,0:T(8,128)(2,1)S(1)}, u32[]{:S(2)}, u32[]{:S(2)}) collective-permute-start(bf16[3,48,768]{2,1,0:T(8,128)(2,1)S(1)} %pad_maximum_fusion.7.refs_1_), channel_id=1, source_target_pairs={{0,4},{4,0},{8,12},{12,8},{16,20},{20,16},{24,28},{28,24},{1,5},{5... | collective-permute-start | bytes 663560 | tf_op jit(solution)/shard_map/ppermute | solution.py:59
  53.4 10.0 %collective-permute-start.15 = (bf16[3,48,768]{2,1,0:T(8,128)(2,1)}, bf16[3,48,768]{2,1,0:T(8,128)(2,1)}, u32[]{:S(2)}, u32[]{:S(2)}) collective-permute-start(bf16[3,48,768]{2,1,0:T(8,128)(2,1)} %collective-permute-done.13.refs_2_), channel_id=1, source_target_pairs={{0,16},{4,12},{8,24},{12,4},{16,0},{20,28},{24,8},{28,20},{1,17},{... | collective-permute-start | bytes 663560 | tf_op jit(solution)/shard_map/ppermute | solution.py:59
  56.3 11.9 %collective-permute-start.3 = (bf16[3,48,768]{2,1,0:T(8,128)(2,1)S(1)}, bf16[3,48,768]{2,1,0:T(8,128)(2,1)}, u32[]{:S(2)}, u32[]{:S(2)}) collective-permute-start(bf16[3,48,768]{2,1,0:T(8,128)(2,1)S(1)} %pad_maximum_fusion.6.refs_1_), channel_id=1, source_target_pairs={{0,8},{4,20},{8,0},{12,28},{16,24},{20,4},{24,16},{28,12},{1,9},{5... | collective-permute-start | bytes 663560 | tf_op jit(solution)/shard_map/ppermute | solution.py:59
  58.7 11.0 %collective-permute-start.17 = (bf16[3,48,768]{2,1,0:T(8,128)(2,1)}, bf16[3,48,768]{2,1,0:T(8,128)(2,1)}, u32[]{:S(2)}, u32[]{:S(2)}) collective-permute-start(bf16[3,48,768]{2,1,0:T(8,128)(2,1)} %collective-permute-done.13.refs_2_), channel_id=1, source_target_pairs={{0,4},{4,0},{8,12},{12,8},{16,20},{20,16},{24,28},{28,24},{1,5},{5... | collective-permute-start | bytes 663560 | tf_op jit(solution)/shard_map/ppermute | solution.py:59
  59.4 10.3 %collective-permute-start.18 = (bf16[3,48,768]{2,1,0:T(8,128)(2,1)}, bf16[3,48,768]{2,1,0:T(8,128)(2,1)}, u32[]{:S(2)}, u32[]{:S(2)}) collective-permute-start(bf16[3,48,768]{2,1,0:T(8,128)(2,1)} %collective-permute-done.14.refs_3_), channel_id=1, source_target_pairs={{0,4},{4,0},{8,12},{12,8},{16,20},{20,16},{24,28},{28,24},{1,5},{5... | collective-permute-start | bytes 663560 | tf_op jit(solution)/shard_map/ppermute | solution.py:59
  63.4 6.9 %collective-permute-start.19 = (bf16[3,48,768]{2,1,0:T(8,128)(2,1)}, bf16[3,48,768]{2,1,0:T(8,128)(2,1)}, u32[]{:S(2)}, u32[]{:S(2)}) collective-permute-start(bf16[3,48,768]{2,1,0:T(8,128)(2,1)} %collective-permute-done.15.refs_4_), channel_id=1, source_target_pairs={{0,4},{4,0},{8,12},{12,8},{16,20},{20,16},{24,28},{28,24},{1,5},{5... | collective-permute-start | bytes 663560 | tf_op jit(solution)/shard_map/ppermute | solution.py:59
  68.2 29.5 %collective-permute-start.4 = (bf16[3,48,768]{2,1,0:T(8,128)(2,1)S(1)}, bf16[3,48,768]{2,1,0:T(8,128)(2,1)}, u32[]{:S(2)}, u32[]{:S(2)}) collective-permute-start(bf16[3,48,768]{2,1,0:T(8,128)(2,1)S(1)} %pad_maximum_fusion.6.refs_1_), channel_id=1, source_target_pairs={{0,16},{4,12},{8,24},{12,4},{16,0},{20,28},{24,8},{28,20},{1,17},{... | collective-permute-start | bytes 663560 | tf_op jit(solution)/shard_map/ppermute | solution.py:59
  69.7 28.6 %collective-permute-start.6 = (bf16[3,48,768]{2,1,0:T(8,128)(2,1)S(1)}, bf16[3,48,768]{2,1,0:T(8,128)(2,1)}, u32[]{:S(2)}, u32[]{:S(2)}) collective-permute-start(bf16[3,48,768]{2,1,0:T(8,128)(2,1)S(1)} %pad_maximum_fusion.6.refs_1_), channel_id=1, source_target_pairs={{0,4},{4,0},{8,12},{12,8},{16,20},{20,16},{24,28},{28,24},{1,5},{5... | collective-permute-start | bytes 663560 | tf_op jit(solution)/shard_map/ppermute | solution.py:59
  69.7 35.2 %collective-permute-start.24 = (bf16[3,192,768]{2,1,0:T(8,128)(2,1)S(1)}, bf16[3,192,768]{2,1,0:T(8,128)(2,1)}, u32[]{:S(2)}, u32[]{:S(2)}) collective-permute-start(bf16[3,192,768]{2,1,0:T(8,128)(2,1)S(1)} %pad_maximum_fusion.1.refs_2_), channel_id=1, source_target_pairs={{0,16},{4,12},{8,24},{12,4},{16,0},{20,28},{24,8},{28,20},{1,17},{... | collective-permute-start | bytes 2654216 | tf_op jit(solution)/shard_map/ppermute | solution.py:59
  70.3 28.1 %collective-permute-start.5 = (bf16[3,48,768]{2,1,0:T(8,128)(2,1)}, bf16[3,48,768]{2,1,0:T(8,128)(2,1)}, u32[]{:S(2)}, u32[]{:S(2)}) collective-permute-start(bf16[3,48,768]{2,1,0:T(8,128)(2,1)} %collective-permute-done.3.refs_2_), channel_id=1, source_target_pairs={{0,16},{4,12},{8,24},{12,4},{16,0},{20,28},{24,8},{28,20},{1,17},{... | collective-permute-start | bytes 663560 | tf_op jit(solution)/shard_map/ppermute | solution.py:59
  77.2 27.9 %collective-permute-start.25 = (bf16[3,192,768]{2,1,0:T(8,128)(2,1)}, bf16[3,192,768]{2,1,0:T(8,128)(2,1)}, u32[]{:S(2)}, u32[]{:S(2)}) collective-permute-start(bf16[3,192,768]{2,1,0:T(8,128)(2,1)} %collective-permute-done.23.refs_3_), channel_id=1, source_target_pairs={{0,16},{4,12},{8,24},{12,4},{16,0},{20,28},{24,8},{28,20},{1,17},{... | collective-permute-start | bytes 2654216 | tf_op jit(solution)/shard_map/ppermute | solution.py:59
  91.8 45.6 %all-to-all-start.1 = ((bf16[4,4,208,256]{3,2,1,0:T(8,128)(2,1)}), bf16[4,4,208,256]{3,2,1,0:T(8,128)(2,1)}, u32[]{:S(2)}, u32[]{:S(2)}) async-start(bf16[4,4,208,256]{3,2,1,0:T(8,128)(2,1)} %get-tuple-element.60), calls=%async_computation.1 | async-start | bytes 3407872 | tf_op jit(solution)/shard_map/all_to_all | solution.py:101
  99.6 18.7 %collective-permute-start.26 = (bf16[3,192,768]{2,1,0:T(8,128)(2,1)S(1)}, bf16[3,192,768]{2,1,0:T(8,128)(2,1)S(1)}, u32[]{:S(2)}, u32[]{:S(2)}) collective-permute-start(bf16[3,192,768]{2,1,0:T(8,128)(2,1)S(1)} %pad_maximum_fusion.1.refs_2_), channel_id=1, source_target_pairs={{0,4},{4,0},{8,12},{12,8},{16,20},{20,16},{24,28},{28,24},{1,5},{5... | collective-permute-start | bytes 2654216 | tf_op jit(solution)/shard_map/ppermute | solution.py:59
  104.6 13.8 %collective-permute-start.27 = (bf16[3,192,768]{2,1,0:T(8,128)(2,1)}, bf16[3,192,768]{2,1,0:T(8,128)(2,1)S(1)}, u32[]{:S(2)}, u32[]{:S(2)}) collective-permute-start(bf16[3,192,768]{2,1,0:T(8,128)(2,1)} %collective-permute-done.23.refs_3_), channel_id=1, source_target_pairs={{0,4},{4,0},{8,12},{12,8},{16,20},{20,16},{24,28},{28,24},{1,5},{5... | collective-permute-start | bytes 2654216 | tf_op jit(solution)/shard_map/ppermute | solution.py:59
  104.9 13.5 %collective-permute-start.28 = (bf16[3,192,768]{2,1,0:T(8,128)(2,1)}, bf16[3,192,768]{2,1,0:T(8,128)(2,1)S(1)}, u32[]{:S(2)}, u32[]{:S(2)}) collective-permute-start(bf16[3,192,768]{2,1,0:T(8,128)(2,1)} %collective-permute-done.24.refs_4_), channel_id=1, source_target_pairs={{0,4},{4,0},{8,12},{12,8},{16,20},{20,16},{24,28},{28,24},{1,5},{5... | collective-permute-start | bytes 2654216 | tf_op jit(solution)/shard_map/ppermute | solution.py:59
  105.1 13.3 %collective-permute-start.29 = (bf16[3,192,768]{2,1,0:T(8,128)(2,1)}, bf16[3,192,768]{2,1,0:T(8,128)(2,1)S(1)}, u32[]{:S(2)}, u32[]{:S(2)}) collective-permute-start(bf16[3,192,768]{2,1,0:T(8,128)(2,1)} %collective-permute-done.25.refs_5_), channel_id=1, source_target_pairs={{0,4},{4,0},{8,12},{12,8},{16,20},{20,16},{24,28},{28,24},{1,5},{5... | collective-permute-start | bytes 2654216 | tf_op jit(solution)/shard_map/ppermute | solution.py:59
  190.1 46.0 %collective-permute-start.50 = (bf16[4,4,192,768]{3,2,0,1:T(8,128)(2,1)}, bf16[4,4,192,768]{3,2,0,1:T(8,128)(2,1)}, u32[]{:S(2)}, u32[]{:S(2)}) collective-permute-start(bf16[4,4,192,768]{3,2,0,1:T(8,128)(2,1)} %copy.119), channel_id=1, source_target_pairs={{0,4},{4,0},{8,12},{12,8},{16,20},{20,16},{24,28},{28,24},{1,5},{5... | collective-permute-start | bytes 14155784 | tf_op jit(solution)/shard_map/ppermute | solution.py:59
  231.0 10.2 %collective-permute-start.30 = (bf16[4,4,48,896]{3,2,0,1:T(8,128)(2,1)}, bf16[4,4,48,896]{3,2,0,1:T(8,128)(2,1)}, u32[]{:S(2)}, u32[]{:S(2)}) collective-permute-start(bf16[4,4,48,896]{3,2,0,1:T(8,128)(2,1)} %copy.107), channel_id=1, source_target_pairs={{0,4},{4,0},{8,12},{12,8},{16,20},{20,16},{24,28},{28,24},{1,5},{5... | collective-permute-start | bytes 4128776 | tf_op jit(solution)/shard_map/ppermute | solution.py:59
  231.5 48.4 %all-to-all-start.2 = ((bf16[4,4,208,256]{3,2,1,0:T(8,128)(2,1)}), bf16[4,4,208,256]{3,2,1,0:T(8,128)(2,1)}, u32[]{:S(2)}, u32[]{:S(2)}) async-start(bf16[4,4,208,256]{3,2,1,0:T(8,128)(2,1)} %get-tuple-element.81), calls=%async_computation.2 | async-start | bytes 3407872 | tf_op jit(solution)/shard_map/all_to_all | solution.py:101
  240.7 53.4 %collective-permute-start.51 = (bf16[2,4,192,768]{3,2,1,0:T(8,128)(2,1)}, bf16[2,4,192,768]{3,2,1,0:T(8,128)(2,1)}, u32[]{:S(2)}, u32[]{:S(2)}) collective-permute-start(bf16[2,4,192,768]{3,2,1,0:T(8,128)(2,1)} %pad_maximum_fusion), channel_id=1, source_target_pairs={{0,16},{4,12},{8,24},{12,4},{16,0},{20,28},{24,8},{28,20},{1,17},{... | collective-permute-start | bytes 7077896 | tf_op jit(solution)/shard_map/ppermute | solution.py:59
  243.5 33.7 %collective-permute-start.31 = (bf16[2,4,48,896]{3,2,1,0:T(8,128)(2,1)}, bf16[2,4,48,896]{3,2,1,0:T(8,128)(2,1)S(1)}, u32[]{:S(2)}, u32[]{:S(2)}) collective-permute-start(bf16[2,4,48,896]{3,2,1,0:T(8,128)(2,1)} %pad_maximum_fusion.2), channel_id=1, source_target_pairs={{0,16},{4,12},{8,24},{12,4},{16,0},{20,28},{24,8},{28,20},{1,17},{... | collective-permute-start | bytes 2064392 | tf_op jit(solution)/shard_map/ppermute | solution.py:59
  279.4 24.2 %collective-permute-start.32 = (bf16[4,48,896]{2,1,0:T(8,128)(2,1)}, bf16[4,48,896]{2,1,0:T(8,128)(2,1)}, u32[]{:S(2)}, u32[]{:S(2)}) collective-permute-start(bf16[4,48,896]{2,1,0:T(8,128)(2,1)} %fusion.10), channel_id=1, source_target_pairs={{0,8},{4,20},{8,0},{12,28},{16,24},{20,4},{24,16},{28,12},{1,9},{5... | collective-permute-start | bytes 1032200 | tf_op jit(solution)/shard_map/ppermute | solution.py:59
  294.2 46.1 %collective-permute-start.40 = (bf16[4,4,48,896]{3,2,0,1:T(8,128)(2,1)}, bf16[4,4,48,896]{3,2,0,1:T(8,128)(2,1)}, u32[]{:S(2)}, u32[]{:S(2)}) collective-permute-start(bf16[4,4,48,896]{3,2,0,1:T(8,128)(2,1)} %copy.112), channel_id=1, source_target_pairs={{0,4},{4,0},{8,12},{12,8},{16,20},{20,16},{24,28},{28,24},{1,5},{5... | collective-permute-start | bytes 4128776 | tf_op jit(solution)/shard_map/ppermute | solution.py:59
  297.6 28.8 %collective-permute-start.52 = (bf16[4,192,768]{2,1,0:T(8,128)(2,1)}, bf16[4,192,768]{2,1,0:T(8,128)(2,1)}, u32[]{:S(2)}, u32[]{:S(2)}) collective-permute-start(bf16[4,192,768]{2,1,0:T(8,128)(2,1)} %fusion), channel_id=1, source_target_pairs={{0,8},{4,20},{8,0},{12,28},{16,24},{20,4},{24,16},{28,12},{1,9},{5... | collective-permute-start | bytes 3538952 | tf_op jit(solution)/shard_map/ppermute | solution.py:59
  300.1 21.3 %all-to-all-start.5 = ((f32[8,4,5376]{2,1,0:T(4,128)}), f32[8,4,5376]{2,1,0:T(4,128)S(1)}, u32[]{:S(2)}, u32[]{:S(2)}) async-start(f32[8,4,5376]{2,1,0:T(4,128)} %broadcast_in_dim.49), calls=%async_computation.5 | async-start | bytes 1376256 | tf_op jit(solution)/shard_map/all_to_all | solution.py:817
  321.3 14.6 %all-to-all-start.3 = ((bf16[4,48,896]{2,1,0:T(8,128)(2,1)}), bf16[4,48,896]{2,1,0:T(8,128)(2,1)S(1)}, u32[]{:S(2)}, u32[]{:S(2)}) async-start(bf16[4,48,896]{2,1,0:T(8,128)(2,1)} %fusion.13), calls=%async_computation.3 | async-start | bytes 688128 | tf_op jit(solution)/shard_map/all_to_all | solution.py:101
  336.7 30.3 %all-to-all-start.7 = ((bf16[4,192,768]{2,1,0:T(8,128)(2,1)}), bf16[4,192,768]{2,1,0:T(8,128)(2,1)S(1)}, u32[]{:S(2)}, u32[]{:S(2)}) async-start(bf16[4,192,768]{2,1,0:T(8,128)(2,1)} %fusion.3), calls=%async_computation.7 | async-start | bytes 2359296 | tf_op jit(solution)/shard_map/all_to_all | solution.py:101
  341.6 11.0 %collective-permute-start.41 = (bf16[2,4,48,896]{3,2,1,0:T(8,128)(2,1)S(1)}, bf16[2,4,48,896]{3,2,1,0:T(8,128)(2,1)S(1)}, u32[]{:S(2)}, u32[]{:S(2)}) collective-permute-start(bf16[2,4,48,896]{3,2,1,0:T(8,128)(2,1)S(1)} %pad_maximum_fusion.3), channel_id=1, source_target_pairs={{0,16},{4,12},{8,24},{12,4},{16,0},{20,28},{24,8},{28,20},{1,17},{... | collective-permute-start | bytes 2064392 | tf_op jit(solution)/shard_map/ppermute | solution.py:59
  353.7 7.7 %collective-permute-start.42 = (bf16[4,48,896]{2,1,0:T(8,128)(2,1)S(1)}, bf16[4,48,896]{2,1,0:T(8,128)(2,1)S(1)}, u32[]{:S(2)}, u32[]{:S(2)}) collective-permute-start(bf16[4,48,896]{2,1,0:T(8,128)(2,1)S(1)} %fusion.6), channel_id=1, source_target_pairs={{0,8},{4,20},{8,0},{12,28},{16,24},{20,4},{24,16},{28,12},{1,9},{5... | collective-permute-start | bytes 1032200 | tf_op jit(solution)/shard_map/ppermute | solution.py:59
  368.0 13.6 %all-to-all-start.4 = ((bf16[4,48,896]{2,1,0:T(8,128)(2,1)}), bf16[4,48,896]{2,1,0:T(8,128)(2,1)S(1)}, u32[]{:S(2)}, u32[]{:S(2)}) async-start(bf16[4,48,896]{2,1,0:T(8,128)(2,1)} %fusion.9), calls=%async_computation.4 | async-start | bytes 688128 | tf_op jit(solution)/shard_map/all_to_all | solution.py:101
  373.1 25.0 %collective-permute-start.53 = (bf16[192,768]{1,0:T(8,128)(2,1)S(1)}, bf16[192,768]{1,0:T(8,128)(2,1)S(1)}, u32[]{:S(2)}, u32[]{:S(2)}) collective-permute-start(bf16[192,768]{1,0:T(8,128)(2,1)S(1)} %reduce_sum.61.refs_0_), channel_id=1, source_target_pairs={{0,8},{4,20},{8,0},{12,28},{16,24},{20,4},{24,16},{28,12},{1,9},{5... | collective-permute-start | bytes 884744 | tf_op jit(solution)/shard_map/ppermute | solution.py:59
  376.7 8.2 %collective-permute-start.33 = (bf16[48,896]{1,0:T(8,128)(2,1)S(1)}, bf16[48,896]{1,0:T(8,128)(2,1)S(1)}, u32[]{:S(2)}, u32[]{:S(2)}) collective-permute-start(bf16[48,896]{1,0:T(8,128)(2,1)S(1)} %reduce_sum.56.refs_0_), channel_id=1, source_target_pairs={{0,8},{4,20},{8,0},{12,28},{16,24},{20,4},{24,16},{28,12},{1,9},{5... | collective-permute-start | bytes 258056 | tf_op jit(solution)/shard_map/ppermute | solution.py:59
  376.7 8.4 %collective-permute-start.34 = (bf16[48,896]{1,0:T(8,128)(2,1)S(1)}, bf16[48,896]{1,0:T(8,128)(2,1)S(1)}, u32[]{:S(2)}, u32[]{:S(2)}) collective-permute-start(bf16[48,896]{1,0:T(8,128)(2,1)S(1)} %reduce_sum.56.refs_0_), channel_id=1, source_target_pairs={{0,16},{4,12},{8,24},{12,4},{16,0},{20,28},{24,8},{28,20},{1,17},{... | collective-permute-start | bytes 258056 | tf_op jit(solution)/shard_map/ppermute | solution.py:59
  376.8 9.9 %collective-permute-start.36 = (bf16[48,896]{1,0:T(8,128)(2,1)S(1)}, bf16[48,896]{1,0:T(8,128)(2,1)S(1)}, u32[]{:S(2)}, u32[]{:S(2)}) collective-permute-start(bf16[48,896]{1,0:T(8,128)(2,1)S(1)} %reduce_sum.56.refs_0_), channel_id=1, source_target_pairs={{0,4},{4,0},{8,12},{12,8},{16,20},{20,16},{24,28},{28,24},{1,5},{5... | collective-permute-start | bytes 258056 | tf_op jit(solution)/shard_map/ppermute | solution.py:59
  381.5 9.1 %all-to-all-start.6 = ((f32[4,1,5376]{2,1,0:T(1,128)}), f32[4,1,5376]{2,1,0:T(1,128)S(1)}, u32[]{:S(2)}, u32[]{:S(2)}) async-start(f32[4,1,5376]{2,1,0:T(1,128)} %copy.117), calls=%async_computation.6 | async-start | bytes 172032 | tf_op jit(solution)/shard_map/all_to_all | solution.py:101
  384.9 5.9 %collective-permute-start.35 = (bf16[48,896]{1,0:T(8,128)(2,1)S(1)}, bf16[48,896]{1,0:T(8,128)(2,1)S(1)}, u32[]{:S(2)}, u32[]{:S(2)}) collective-permute-start(bf16[48,896]{1,0:T(8,128)(2,1)S(1)} %collective-permute-done.33.refs_1_), channel_id=1, source_target_pairs={{0,16},{4,12},{8,24},{12,4},{16,0},{20,28},{24,8},{28,20},{1,17},{... | collective-permute-start | bytes 258056 | tf_op jit(solution)/shard_map/ppermute | solution.py:59
  385.1 5.7 %collective-permute-start.37 = (bf16[48,896]{1,0:T(8,128)(2,1)S(1)}, bf16[48,896]{1,0:T(8,128)(2,1)S(1)}, u32[]{:S(2)}, u32[]{:S(2)}) collective-permute-start(bf16[48,896]{1,0:T(8,128)(2,1)S(1)} %collective-permute-done.33.refs_1_), channel_id=1, source_target_pairs={{0,4},{4,0},{8,12},{12,8},{16,20},{20,16},{24,28},{28,24},{1,5},{5... | collective-permute-start | bytes 258056 | tf_op jit(solution)/shard_map/ppermute | solution.py:59
  385.1 6.2 %collective-permute-start.38 = (bf16[48,896]{1,0:T(8,128)(2,1)S(1)}, bf16[48,896]{1,0:T(8,128)(2,1)S(1)}, u32[]{:S(2)}, u32[]{:S(2)}) collective-permute-start(bf16[48,896]{1,0:T(8,128)(2,1)S(1)} %collective-permute-done.34.refs_2_), channel_id=1, source_target_pairs={{0,4},{4,0},{8,12},{12,8},{16,20},{20,16},{24,28},{28,24},{1,5},{5... | collective-permute-start | bytes 258056 | tf_op jit(solution)/shard_map/ppermute | solution.py:59
  386.7 6.8 %collective-permute-start.43 = (bf16[48,896]{1,0:T(8,128)(2,1)S(1)}, bf16[48,896]{1,0:T(8,128)(2,1)S(1)}, u32[]{:S(2)}, u32[]{:S(2)}) collective-permute-start(bf16[48,896]{1,0:T(8,128)(2,1)S(1)} %reduce_sum.57.refs_8_), channel_id=1, source_target_pairs={{0,8},{4,20},{8,0},{12,28},{16,24},{20,4},{24,16},{28,12},{1,9},{5... | collective-permute-start | bytes 258056 | tf_op jit(solution)/shard_map/ppermute | solution.py:59
  390.8 4.6 %collective-permute-start.44 = (bf16[48,896]{1,0:T(8,128)(2,1)S(1)}, bf16[48,896]{1,0:T(8,128)(2,1)S(1)}, u32[]{:S(2)}, u32[]{:S(2)}) collective-permute-start(bf16[48,896]{1,0:T(8,128)(2,1)S(1)} %reduce_sum.57.refs_8_), channel_id=1, source_target_pairs={{0,16},{4,12},{8,24},{12,4},{16,0},{20,28},{24,8},{28,20},{1,17},{... | collective-permute-start | bytes 258056 | tf_op jit(solution)/shard_map/ppermute | solution.py:59
  391.4 6.7 %collective-permute-start.46 = (bf16[48,896]{1,0:T(8,128)(2,1)S(1)}, bf16[48,896]{1,0:T(8,128)(2,1)S(1)}, u32[]{:S(2)}, u32[]{:S(2)}) collective-permute-start(bf16[48,896]{1,0:T(8,128)(2,1)S(1)} %reduce_sum.57.refs_8_), channel_id=1, source_target_pairs={{0,4},{4,0},{8,12},{12,8},{16,20},{20,16},{24,28},{28,24},{1,5},{5... | collective-permute-start | bytes 258056 | tf_op jit(solution)/shard_map/ppermute | solution.py:59
  393.5 4.5 %collective-permute-start.45 = (bf16[48,896]{1,0:T(8,128)(2,1)S(1)}, bf16[48,896]{1,0:T(8,128)(2,1)S(1)}, u32[]{:S(2)}, u32[]{:S(2)}) collective-permute-start(bf16[48,896]{1,0:T(8,128)(2,1)S(1)} %collective-permute-done.43.refs_9_), channel_id=1, source_target_pairs={{0,16},{4,12},{8,24},{12,4},{16,0},{20,28},{24,8},{28,20},{1,17},{... | collective-permute-start | bytes 258056 | tf_op jit(solution)/shard_map/ppermute | solution.py:59
  394.2 15.2 %collective-permute-start.47 = (bf16[48,896]{1,0:T(8,128)(2,1)S(1)}, bf16[48,896]{1,0:T(8,128)(2,1)S(1)}, u32[]{:S(2)}, u32[]{:S(2)}) collective-permute-start(bf16[48,896]{1,0:T(8,128)(2,1)S(1)} %collective-permute-done.43.refs_9_), channel_id=1, source_target_pairs={{0,4},{4,0},{8,12},{12,8},{16,20},{20,16},{24,28},{28,24},{1,5},{5... | collective-permute-start | bytes 258056 | tf_op jit(solution)/shard_map/ppermute | solution.py:59
  395.4 14.0 %collective-permute-start.48 = (bf16[48,896]{1,0:T(8,128)(2,1)S(1)}, bf16[48,896]{1,0:T(8,128)(2,1)S(1)}, u32[]{:S(2)}, u32[]{:S(2)}) collective-permute-start(bf16[48,896]{1,0:T(8,128)(2,1)S(1)} %collective-permute-done.44.refs_10_), channel_id=1, source_target_pairs={{0,4},{4,0},{8,12},{12,8},{16,20},{20,16},{24,28},{28,24},{1,5},{5... | collective-permute-start | bytes 258056 | tf_op jit(solution)/shard_map/ppermute | solution.py:59
  398.0 12.4 %collective-permute-start.49 = (bf16[48,896]{1,0:T(8,128)(2,1)S(1)}, bf16[48,896]{1,0:T(8,128)(2,1)S(1)}, u32[]{:S(2)}, u32[]{:S(2)}) collective-permute-start(bf16[48,896]{1,0:T(8,128)(2,1)S(1)} %collective-permute-done.45.refs_11_), channel_id=1, source_target_pairs={{0,4},{4,0},{8,12},{12,8},{16,20},{20,16},{24,28},{28,24},{1,5},{5... | collective-permute-start | bytes 258056 | tf_op jit(solution)/shard_map/ppermute | solution.py:59
  398.0 11.8 %collective-permute-start.54 = (bf16[192,768]{1,0:T(8,128)(2,1)S(1)}, bf16[192,768]{1,0:T(8,128)(2,1)S(1)}, u32[]{:S(2)}, u32[]{:S(2)}) collective-permute-start(bf16[192,768]{1,0:T(8,128)(2,1)S(1)} %reduce_sum.61.refs_0_), channel_id=1, source_target_pairs={{0,16},{4,12},{8,24},{12,4},{16,0},{20,28},{24,8},{28,20},{1,17},{... | collective-permute-start | bytes 884744 | tf_op jit(solution)/shard_map/ppermute | solution.py:59
  398.0 11.9 %collective-permute-start.55 = (bf16[192,768]{1,0:T(8,128)(2,1)S(1)}, bf16[192,768]{1,0:T(8,128)(2,1)S(1)}, u32[]{:S(2)}, u32[]{:S(2)}) collective-permute-start(bf16[192,768]{1,0:T(8,128)(2,1)S(1)} %collective-permute-done.53.refs_1_), channel_id=1, source_target_pairs={{0,16},{4,12},{8,24},{12,4},{16,0},{20,28},{24,8},{28,20},{1,17},{... | collective-permute-start | bytes 884744 | tf_op jit(solution)/shard_map/ppermute | solution.py:59
  409.3 4.1 collective-permute-start.56
  409.4 4.1 collective-permute-start.57
  409.9 3.6 collective-permute-start.58
  409.9 3.5 collective-permute-start.59
  (48 other events, 455.0 us)
